TPU v7x, 32 devices: a whole 2x2x4 slice. The times are simulated.
32 devices in a mesh: ep: 16 (over z, y, x), os: 2 (over core).
Axes of the slice: x: 2, y: 2, z: 4, core: 2. Of those that a mesh axis runs over, the one named last changes fastest.
Arguments:
- tokens: bfloat16 [2048, 2048], P('ep', 'os'), may hold values from -6 to 6
- cotangent: bfloat16 [2048, 2048], P('ep', 'os'), may hold values from -6 to 6
- expert_ids: int32 [2048, 8], P('ep'), may hold values from 0 to 15, all different within a row; in each aligned block of 128 rows (0 to 127, 128 to 255, ...) at most 96 rows name the same one
- route_weight: float32 [2048, 8], P('ep'), may hold values from 0.1 to 1
- placement: int32 [16], replicated, may hold values from 0 to 15, each once
- swap_flags: int32 [2, 16], replicated, may hold values from 0 to 1, as said below
- params: bfloat16 [16, 3, 2048, 384], P('ep', None, 'os'), may hold values from -1 to 1
- first_moment: bfloat16 [16, 3, 2048, 384], P('ep', None, 'os'), may hold values from -6 to 6
- second_moment: bfloat16 [16, 3, 2048, 384], P('ep', None, 'os'), may hold values from 0.5 to 20
Outputs:
- mixed: bfloat16 [2048, 2048], P('ep', 'os')
- input_grad: bfloat16 [2048, 2048], P('ep', 'os')
- new_params: bfloat16 [16, 3, 2048, 384], P('ep', None, 'os')
- new_first: bfloat16 [16, 3, 2048, 384], P('ep', None, 'os')
- new_second: bfloat16 [16, 3, 2048, 384], P('ep', None, 'os')
Inputs may be any that keep to these rules, and one draw needn't show every extreme that they name: `expert_ids`: each row names 8 different experts; in each aligned block of 128 rows (the rows of one index of ep) no expert is named by more than 96 rows, a bound that some block reaches. `placement`: A permutation of the 16 expert ids. swap_flags[r, i] = swap_flags[r, i XOR 2^b_r] with b_0 = log2(16) - 1 and b_1 = 0.
All inputs are finite; a program needn't handle non-finite values.
Results may differ from a plain program's by a relative error of at most 0.023.
Values may be sent and summed in bfloat16 or wider, within the bound.
No kernel may reach another device: no remote copies, remote signals or barrier semaphores. Data moves between devices by JAX's collectives and lax.ppermute only.
A program may use at most 128 MiB of HBM per device.

v0:
```python
import jax
import jax.numpy as jnp
from jax import lax
from jax.experimental import pallas as pl
from jax.experimental.pallas import tpu as pltpu
from jax.sharding import PartitionSpec as P

beta_first = 0.9
beta_second = 0.999
learn_rate = 0.01
adam_eps = 1e-08
adam_count = 10.0


def both(first, second):
    return lax.optimization_barrier((first, second))


def permute(value, pairs):
    return lax.ppermute(value, "ep", pairs)


def from_partner(value, bit):
    return permute(value, [(i, i ^ bit) for i in range(lax.axis_size("ep"))])


def over_cores(value):
    if lax.axis_size("os") != 2:
        return (lax.psum(value, "os"),)
    return value, lax.ppermute(value, "os", [(0, 1), (1, 0)])


def adam_kernel(weight, moments, grad_gate, grad_up, grad_down, new_weight, new_first, new_second):
    for k, grad_ref in enumerate((grad_gate, grad_up, grad_down)):
        grad = grad_ref[...]
        first = beta_first * moments[0, k].astype(jnp.float32) + (1.0 - beta_first) * grad
        second = (
            beta_second * moments[0, 3 + k].astype(jnp.float32) + (1.0 - beta_second) * grad * grad
        )
        step = (learn_rate / (1.0 - beta_first**adam_count)) * first
        size = jnp.sqrt((1.0 / (1.0 - beta_second**adam_count)) * second) + adam_eps
        new_weight[0, k] = (weight[k].astype(jnp.float32) - step / size).astype(jnp.bfloat16)
        new_first[0, k] = first.astype(jnp.bfloat16)
        new_second[0, k] = second.astype(jnp.bfloat16)


def adam_update(weight, moments, grad):
    _, rows, width = weight.shape
    parts = 8 if rows % 128 == 0 else 4
    size = rows // parts
    per_quarter = parts // 4
    state = jax.ShapeDtypeStruct((1, 3, rows, width), jnp.bfloat16)
    return pl.pallas_call(
        adam_kernel,
        out_shape=(state,) * 3,
        grid=(parts,),
        in_specs=[
            pl.BlockSpec((3, size, width), lambda i: (0, i, 0)),
            pl.BlockSpec(
                (1, 6, size, width), lambda i: (i // per_quarter, 0, i % per_quarter, 0)
            ),
        ]
        + [pl.BlockSpec((size, width), lambda i: (i, 0))] * 3,
        out_specs=(pl.BlockSpec((1, 3, size, width), lambda i: (0, 0, i, 0)),) * 3,
        compiler_params=pltpu.CompilerParams(vmem_limit_bytes=32 * 1024 * 1024),
        cost_estimate=pl.CostEstimate(
            flops=40 * weight.size, transcendentals=2 * weight.size, bytes_accessed=16 * weight.size
        ),
    )(weight, moments, *grad)


def high_bits(experts):
    return [1 << b for b in range(experts.bit_length() - 2, 1, -1)]


def add_rounded(*parts):
    total = parts[0].astype(jnp.float32)
    for part in parts[1:]:
        total = total + part.astype(jnp.float32)
    return total.astype(jnp.bfloat16)


def planes():
    return [[i, i + 1, i + 2, i + 3] for i in range(0, lax.axis_size("ep"), 4)]


class Migration:
    def __init__(self, flags):
        mine = lax.axis_index("ep")
        self.mate = mate = mine & 3
        near = lax.dynamic_slice_in_dim(flags, mine - mate, 4, axis=1)
        index = jnp.arange(4, dtype=jnp.int32)
        swaps, turns = near[0], near[1]
        rank = jnp.sum(jnp.where(index[None, :] < index[:, None], swaps[None, :], 0), axis=1)
        chosen = (rank[None, :] == index[:, None]) & (swaps[None, :] == 1)
        active = jnp.sum(jnp.where(chosen, index[None, :], 0), axis=1)
        source = index ^ turns
        at_source = source[:, None] == index[None, :]
        swapped = jnp.sum(jnp.where(at_source, swaps[None, :], 0), axis=1)
        place = jnp.sum(jnp.where(at_source, rank[None, :], 0), axis=1)
        self.facts = jnp.concatenate((active, source, place, swapped))


def quartered(array):
    k, rows, width = array.shape
    return array.reshape(k, 4, rows // 4, width).transpose(1, 0, 2, 3)


def spread(quarters):
    return lax.all_to_all(quarters, "ep", 0, 0, tiled=True, axis_index_groups=planes())


def to_cross(facts, pool):
    block = (1,) + pool.shape[1:]

    def kernel(facts, pool, three, fourth):
        slot = pl.program_id(0)

        @pl.when(slot < 3)
        def _():
            three[...] = pool[...]

        @pl.when(slot == 3)
        def _():
            fourth[...] = pool[...]

    return pl.pallas_call(
        kernel,
        out_shape=tuple(
            jax.ShapeDtypeStruct((slots,) + pool.shape[1:], pool.dtype) for slots in (3, 1)
        ),
        grid_spec=pltpu.PrefetchScalarGridSpec(
            num_scalar_prefetch=1,
            grid=(4,),
            in_specs=[pl.BlockSpec(block, lambda i, facts: (facts[i], 0, 0, 0))],
            out_specs=(
                pl.BlockSpec(block, lambda i, facts: (jnp.minimum(i, 2), 0, 0, 0)),
                pl.BlockSpec(block, lambda i, facts: (0, 0, 0, 0)),
            ),
        ),
        compiler_params=pltpu.CompilerParams(vmem_limit_bytes=32 * 1024 * 1024),
        cost_estimate=pl.CostEstimate(flops=0, transcendentals=0, bytes_accessed=4 * pool.size),
    )(facts, pool)


def across(going):
    return from_partner(going, lax.axis_size("ep") // 2)


def fourth_across(full, going):
    return lax.cond(full, across, lambda going: going, going)


def pick(facts, pool, came, fourth, *picked):
    k = came.shape[1]
    rest = came.shape[2:]
    ahead = len(picked) * k

    def kernel(facts, pool, came, fourth, *refs):
        out = refs[-1]
        dest = pl.program_id(0)
        swapped = facts[12 + dest] == 1
        last = facts[8 + dest] == 3

        @pl.when(swapped & jnp.logical_not(last))
        def _():
            out[:, ahead:] = came[...]

        @pl.when(swapped & last)
        def _():
            out[:, ahead:] = fourth[...]

        @pl.when(jnp.logical_not(swapped))
        def _():
            out[:, ahead:] = pool[...]

        for i in range(len(picked)):
            out[:, i * k : (i + 1) * k] = refs[i][...]

    block = (1, k) + rest
    width = ahead + k
    return pl.pallas_call(
        kernel,
        out_shape=jax.ShapeDtypeStruct((4, width) + rest, came.dtype),
        grid_spec=pltpu.PrefetchScalarGridSpec(
            num_scalar_prefetch=1,
            grid=(4,),
            in_specs=[
                pl.BlockSpec(block, lambda i, facts: (facts[4 + i], 0, 0, 0)),
                pl.BlockSpec(block, lambda i, facts: (jnp.minimum(facts[8 + i], 2), 0, 0, 0)),
                pl.BlockSpec(block, lambda i, facts: (0, 0, 0, 0)),
            ]
            + [pl.BlockSpec(block, lambda i, facts: (i, 0, 0, 0))] * len(picked),
            out_specs=pl.BlockSpec((1, width) + rest, lambda i, facts: (i, 0, 0, 0)),
        ),
        compiler_params=pltpu.CompilerParams(vmem_limit_bytes=32 * 1024 * 1024),
        cost_estimate=pl.CostEstimate(
            flops=0, transcendentals=0, bytes_accessed=2 * (2 * width + k) * pool[:, 0].size
        ),
    )(facts, pool, came, fourth, *picked)


def assemble_rows(tok_rows, blocks):
    n, rows, shard = blocks[0].shape
    parts = ((0, tok_rows), (tok_rows, tok_rows), (2 * tok_rows, rows - 2 * tok_rows))

    def kernel(*refs):
        sources, outs, sems = refs[: len(blocks)], refs[len(blocks) : -1], refs[-1]
        copies = [
            pltpu.make_async_copy(
                source.at[:, pl.ds(start, size)], out.at[pl.ds(i * n, n)], sems.at[i, p]
            )
            for i, source in enumerate(sources)
            for p, ((start, size), out) in enumerate(zip(parts, outs))
        ]
        for copy in copies:
            copy.start()
        for copy in copies:
            copy.wait()

    return pl.pallas_call(
        kernel,
        out_shape=tuple(
            jax.ShapeDtypeStruct((len(blocks) * n, size, shard), blocks[0].dtype) for _, size in parts
        ),
        in_specs=[pl.BlockSpec(memory_space=pl.ANY)] * len(blocks),
        out_specs=(pl.BlockSpec(memory_space=pltpu.VMEM),) * 3,
        scratch_shapes=[pltpu.SemaphoreType.DMA((len(blocks), 3))],
        compiler_params=pltpu.CompilerParams(vmem_limit_bytes=32 * 1024 * 1024),
        cost_estimate=pl.CostEstimate(
            flops=0, transcendentals=0, bytes_accessed=4 * len(blocks) * blocks[0].size
        ),
    )(*blocks)


def partial_kernel(x_rows, dy_rows, weight, out):
    for k, rows in enumerate((x_rows, x_rows, dy_rows)):
        out[k] = jnp.dot(rows[...], weight[k], preferred_element_type=jnp.float32).astype(
            jnp.bfloat16
        )


def partial_products(x_rows, dy_rows, weight):
    rows, shard = x_rows.shape
    width = weight.shape[-1]
    size = 256
    return pl.pallas_call(
        partial_kernel,
        out_shape=jax.ShapeDtypeStruct((3, rows, width), jnp.bfloat16),
        grid=(rows // size,),
        in_specs=[
            pl.BlockSpec((size, shard), lambda i: (i, 0)),
            pl.BlockSpec((size, shard), lambda i: (i, 0)),
            pl.BlockSpec((3, shard, width), lambda i: (0, 0, 0)),
        ],
        out_specs=pl.BlockSpec((3, size, width), lambda i: (0, i, 0)),
        compiler_params=pltpu.CompilerParams(vmem_limit_bytes=32 * 1024 * 1024),
        cost_estimate=pl.CostEstimate(
            flops=6 * rows * shard * width,
            transcendentals=0,
            bytes_accessed=2 * (2 * rows * shard + 3 * shard * width + 3 * rows * width),
        ),
    )(x_rows, dy_rows, weight)


def middle_kernel(*refs):
    *addends, scale, down, hidden_ref, d_gate_ref, d_up_ref, left, right = refs

    def total(k):
        value = addends[0][k].astype(jnp.float32)
        for addend in addends[1:]:
            value = value + addend[k].astype(jnp.float32)
        return value

    gate, up, back = total(0), total(1), total(2)
    sigma = jax.nn.sigmoid(gate)
    active = gate * sigma
    hidden = (active * up).astype(jnp.bfloat16)
    hidden_ref[...] = hidden
    d_gate_ref[...] = (back * up * sigma * (1.0 + gate * (1.0 - sigma))).astype(jnp.bfloat16)
    d_up_ref[...] = (back * active).astype(jnp.bfloat16)
    half = left.shape[1]
    for part, out in enumerate((left, right)):
        rows_out = lax.dot_general(
            hidden,
            down[0, part * half : (part + 1) * half],
            (((1,), (1,)), ((), ())),
            preferred_element_type=jnp.float32,
        )
        out[...] = (scale[...] * rows_out).astype(jnp.bfloat16)


def middle(addends, scale, weight):
    _, rows, width = addends[0].shape
    shard = weight.shape[1]
    size = 256
    narrow = jax.ShapeDtypeStruct((rows, width), jnp.bfloat16)
    wide = jax.ShapeDtypeStruct((rows, shard // 2), jnp.bfloat16)
    return pl.pallas_call(
        middle_kernel,
        out_shape=(narrow,) * 3 + (wide,) * 2,
        grid=(rows // size,),
        in_specs=[pl.BlockSpec((3, size, width), lambda i: (0, i, 0))] * len(addends)
        + [
            pl.BlockSpec((size, 1), lambda i: (i, 0)),
            pl.BlockSpec((1, shard, width), lambda i: (2, 0, 0)),
        ],
        out_specs=(pl.BlockSpec((size, width), lambda i: (i, 0)),) * 3
        + (pl.BlockSpec((size, shard // 2), lambda i: (i, 0)),) * 2,
        compiler_params=pltpu.CompilerParams(vmem_limit_bytes=32 * 1024 * 1024),
        cost_estimate=pl.CostEstimate(
            flops=2 * rows * shard * width,
            transcendentals=rows * width,
            bytes_accessed=2 * (9 * rows * width + rows * shard + shard * width),
        ),
    )(*addends, scale, weight)


def collect(quarters):
    quarters = lax.all_to_all(quarters, "ep", 0, 0, tiled=True, axis_index_groups=planes())
    quarters = quarters.transpose(1, 0, 2, 3)
    return quarters.reshape(quarters.shape[0], -1, quarters.shape[-1])


def scatter_plane(left, right, ahead=()):
    size, half = left.shape[0] // 4, left.shape[1]
    left_out, right_out = left[size : 3 * size], right[2 * size :]
    if ahead:
        left_out, right_out, *ahead = lax.optimization_barrier((left_out, right_out, *ahead))
    return left, right, from_partner(left_out, 1), from_partner(right_out, 2), ahead


def scatter_plane_end(left, right, left_in, right_in):
    size = left.shape[0] // 4
    left_last = from_partner(add_rounded(left[3 * size :], left_in[size:]), 2)
    right_last = from_partner(add_rounded(right[size : 2 * size], right_in[:size]), 1)
    left = add_rounded(left[:size], left_in[:size], left_last)
    right = add_rounded(right[:size], right_in[size:], right_last)
    return jnp.concatenate((left, right), axis=1)


def scatter_rest(block):
    for bit in reversed(high_bits(lax.axis_size("ep"))):
        keep = block.shape[0] // 2
        block = add_rounded(block[:keep], from_partner(block[keep:], bit))
    return block


def dot(a, b, dims):
    return lax.dot_general(a, b, ((dims[:1], dims[1:]), ((), ())), preferred_element_type=jnp.float32)


def on_device(
    tokens,
    cotangent,
    expert_ids,
    route_weight,
    placement,
    swap_flags,
    params,
    first_moment,
    second_moment,
):
    experts = lax.axis_size("ep")
    mine = lax.axis_index("ep")
    index = jnp.arange(experts, dtype=jnp.int32)
    table = jnp.sum(
        jnp.where(
            expert_ids.T[None, :, :] == index[:, None, None], route_weight.T[None, :, :], 0.0
        ),
        axis=1,
    )
    tok_rows, shard = tokens.shape
    half = shard // 2
    far = experts // 2

    def group(part, *operands):
        if lax.axis_size("os") != 2:
            return part(*operands)
        shapes = jax.eval_shape(part, *operands)
        return lax.cond(
            swap_flags[0, 0] >= 0,
            part,
            lambda *_: jax.tree.map(lambda x: jnp.zeros(x.shape, x.dtype), shapes),
            *operands,
        )

    terms = []
    for _ in range(3):
        terms.append(lax.reduce_precision(table, 8, 7))
        table = table - terms[-1]
    terms = jnp.stack(terms).astype(jnp.bfloat16).reshape(-1, shard)
    used = terms.shape[0]
    terms = jnp.pad(terms, ((0, -used % 16), (0, 0)))
    block = jnp.concatenate((tokens, cotangent, terms))[None]

    bits = high_bits(experts)

    def over_z(block, params):
        parts = [block]
        for bit in bits[:-1]:
            parts = parts + [from_partner(part, bit) for part in parts]
        other = jnp.concatenate([from_partner(part, bits[-1]) for part in parts])
        block = jnp.concatenate(parts)
        one, two = from_partner(block, 1), from_partner(block, 2)
        pool = spread(quartered(params))
        facts = Migration(swap_flags).facts
        place = placement
        for rnd, bit in enumerate((experts // 2, 1)):
            place = jnp.where(swap_flags[rnd] == 1, place[index ^ bit], place)
        facts = jnp.concatenate((facts, place[mine][None]))
        full = jnp.any(jnp.sum(swap_flags[0].reshape(-1, 4), axis=1) > 3)
        return block, other, one, two, pool, to_cross(facts, pool), facts, full

    block, other, one, two, w_pool, w_going, facts, full = group(over_z, block, params[0])

    w_three, w_fourth = w_going
    w_came = across(w_three)

    def to_neighbours(other, one, two, first_moment):
        three = from_partner(two, 1)
        other_one, other_two = from_partner(other, 1), from_partner(other, 2)
        other_three = from_partner(other_one, 2)
        pool = spread(quartered(first_moment))
        return three, other_one, other_two, other_three, pool, to_cross(facts, pool)

    three, other_one, other_two, other_three, m_pool, (m_three, m_fourth) = group(
        to_neighbours, other, one, two, first_moment[0]
    )
    w_came, w_fourth = both(w_came, w_fourth)
    w_fourth = fourth_across(full, w_fourth)
    w_fourth, m_three = both(w_fourth, m_three)
    m_came = across(m_three)

    def assemble(w_pool, w_came, w_fourth, second_moment, *blocks):
        x_rows, dy_rows, terms = assemble_rows(tok_rows, blocks)
        weight = collect(pick(facts, w_pool, w_came, w_fourth))
        terms = terms[:, :used].reshape(-1, 3, experts, tok_rows)
        terms = lax.dynamic_index_in_dim(terms, facts[16], axis=2, keepdims=False)
        scale = jnp.sum(terms.astype(jnp.float32), axis=1).reshape(-1, 1)
        dy_rows = dy_rows.reshape(-1, shard).astype(jnp.float32)
        dy_rows = (scale * dy_rows).astype(jnp.bfloat16)
        return weight, x_rows.reshape(-1, shard), dy_rows, scale, quartered(second_moment)

    weight, x_rows, dy_rows, scale, v_quarters = group(
        assemble, w_pool, w_came, w_fourth, second_moment[0],
        block, other, one, other_one, three, other_three, two, other_two,
    )
    def forward(weight, x_rows, dy_rows, scale, v_quarters):
        pool = spread(v_quarters)
        addends = group(over_cores, partial_products(x_rows, dy_rows, weight))
        hidden, d_gate, d_up, *mixed_rows = middle(addends, scale, weight)
        return hidden, d_gate, d_up, mixed_rows, pool

    hidden, d_gate, d_up, mixed_rows, v_pool = group(
        forward, weight, x_rows, dy_rows, scale, v_quarters
    )
    v_three, v_fourth = group(lambda pool: to_cross(facts, pool), v_pool)
    m_came, m_fourth = both(m_came, m_fourth)
    m_fourth = fourth_across(full, m_fourth)
    m_fourth, v_three = both(m_fourth, v_three)
    v_came = across(v_three)

    def backward(weight, x_rows, dy_rows, hidden, d_gate, d_up, mixed_rows, m_pool, m_came, m_fourth):
        left, right, left_in, right_in, _ = scatter_plane(*mixed_rows)
        grad_rows = [
            (dot(d_gate, weight[0, part], (1, 1)) + dot(d_up, weight[1, part], (1, 1))).astype(
                jnp.bfloat16
            )
            for part in (slice(0, half), slice(half, shard))
        ]
        *gone, (left_in, right_in) = scatter_plane(*grad_rows, ahead=(left_in, right_in))
        mixed = scatter_plane_end(left, right, left_in, right_in)
        input_grad = scatter_plane_end(*gone)
        grad = (
            dot(x_rows, d_gate, (0, 0)),
            dot(x_rows, d_up, (0, 0)),
            dot(dy_rows, hidden, (0, 0)),
        )
        return mixed, input_grad, grad, pick(facts, m_pool, m_came, m_fourth)

    mixed, input_grad, grad, m_picked = group(
        backward, weight, x_rows, dy_rows, hidden, d_gate, d_up, mixed_rows, m_pool, m_came, m_fourth
    )
    v_came, v_fourth = both(v_came, v_fourth)
    v_fourth = fourth_across(full, v_fourth)

    def to_owners(mixed, input_grad, m_picked, v_pool, v_came, v_fourth):
        moments = lax.all_to_all(
            pick(facts, v_pool, v_came, v_fourth, m_picked),
            "ep",
            0,
            0,
            tiled=True,
            axis_index_groups=planes(),
        )
        return scatter_rest(mixed), scatter_rest(input_grad), moments

    mixed, input_grad, moments = group(
        to_owners, mixed, input_grad, m_picked, v_pool, v_came, v_fourth
    )
    return (mixed, input_grad, *adam_update(weight, moments, grad))


def solution(mesh):
    state = P("ep", None, "os", None)
    rows = P("ep", "os")
    return jax.shard_map(
        on_device,
        mesh=mesh,
        in_specs=(rows, rows, P("ep", None), P("ep", None), P(), P(), state, state, state),
        out_specs=(rows, rows, state, state, state),
        check_vma=False,
    )
```

profile of v0, /device:TPU:0, one launch (start us, length us, event | category | flops | bytes accessed | tf_op | source)
XLA Modules:
  0.0 391.0 jit_solution(8084190993008881260)
XLA Ops:
  2.7 65.5 %conditional.11 = (bf16[2,272,1024]{2,1,0:T(8,128)(2,1)}, bf16[2,272,1024]{2,1,0:T(8,128)(2,1)S(1)}, bf16[2,272,1024]{2,1,0:T(8,128)(2,1)}, bf16[2,272,1024]{2,1...) conditional(s32[]{:T(128)} %bitcast.24, () %tuple.99, ...), branch_computations={%region_1.2_spmd, %region_2.9_spmd} | conditional | flops 1116582 | bytes 36579772 | solution.py:381
  2.7 4.1 %collective-permute-start.12 = (bf16[1,272,1024]{2,1,0:T(8,128)(2,1)S(1)}, bf16[1,272,1024]{2,1,0:T(8,128)(2,1)S(1)}, u32[]{:S(2)}, u32[]{:S(2)}) collective-permute-start(bf16[1,272,1024]{2,1,0:T(8,128)(2,1)S(1)} %bitcast.69), channel_id=1, source_target_pairs={{0,16},{2,18},{4,20},{6,22},{8,24},{10,26},{12,28},{14,30},{16,0},... | collective-permute-start | bytes 1671176 | tf_op jit(solution)/shard_map/cond/branch_1_fun/ppermute | solution.py:20
  6.8 1.6 collective-permute-start.13
  8.4 3.3 copy.39
  11.7 4.5 %all-to-all-start.4 = ((bf16[4,3,256,384]{3,2,1,0:T(8,128)(2,1)}), bf16[4,3,256,384]{3,2,1,0:T(8,128)(2,1)}, u32[]{:S(2)}, u32[]{:S(2)}) async-start(bf16[4,3,256,384]{3,2,1,0:T(8,128)(2,1)} %bitcast.63), calls=%async_computation.4 | async-start | bytes 4718592 | tf_op jit(solution)/shard_map/cond/branch_1_fun/all_to_all | solution.py:110
  18.5 13.0 %collective-permute-done.12 = bf16[1,272,1024]{2,1,0:T(8,128)(2,1)S(1)} collective-permute-done((bf16[1,272,1024]{2,1,0:T(8,128)(2,1)S(1)}, bf16[1,272,1024]{2,1,0:T(8,128)(2,1)S(1)}, u32[]{:S(2)}, u32[]{:S(2)}) %collective-permute-start.12) | collective-permute-done | bytes 557088 | tf_op jit(solution)/shard_map/cond/branch_1_fun/ppermute | solution.py:20
  32.6 1.5 collective-permute-start.15
  34.1 1.5 collective-permute-start.16
  38.5 10.1 %collective-permute-done.14 = bf16[1,272,1024]{2,1,0:T(8,128)(2,1)S(1)} collective-permute-done((bf16[1,272,1024]{2,1,0:T(8,128)(2,1)S(1)}, bf16[1,272,1024]{2,1,0:T(8,128)(2,1)S(1)}, u32[]{:S(2)}, u32[]{:S(2)}) %collective-permute-start.14) | collective-permute-done | bytes 557088 | tf_op jit(solution)/shard_map/cond/branch_1_fun/ppermute | solution.py:20
  48.7 4.8 %branch_1_fun.9 = (bf16[3,3,256,384]{3,2,1,0:T(8,128)(2,1)}, bf16[1,3,256,384]{3,2,1,0:T(8,128)(2,1)}) custom-call(s32[17]{0:T(128)} %concatenate.14.facts, bf16[4,3,256,384]{3,2,1,0:T(8,128)(2,1)} %all-to-all-done.4.pool), custom_call_target="tpu_custom_call" | custom-call | bytes 4718592 | tf_op jit(solution)/shard_map/cond/branch_1_fun/pallas_call | solution.py:127
  53.5 14.1 %collective-permute-done.15 = bf16[2,272,1024]{2,1,0:T(8,128)(2,1)} collective-permute-done((bf16[2,272,1024]{2,1,0:T(8,128)(2,1)}, bf16[2,272,1024]{2,1,0:T(8,128)(2,1)}, u32[]{:S(2)}, u32[]{:S(2)}) %collective-permute-start.15) | collective-permute-done | bytes 1114144 | tf_op jit(solution)/shard_map/cond/branch_1_fun/ppermute | solution.py:20
  68.6 84.7 %conditional.13 = (bf16[2,272,1024]{2,1,0:T(8,128)(2,1)}, bf16[2,272,1024]{2,1,0:T(8,128)(2,1)}, bf16[2,272,1024]{2,1,0:T(8,128)(2,1)}, bf16[2,272,1024]{2,1,0:T...) conditional(s32[]{:T(128)} %bitcast.24, () %tuple.102, ...), branch_computations={%region_9.10_spmd, %region_10.11_spmd} | conditional | bytes 34341112 | solution.py:381
  70.1 3.3 copy.38
  73.4 4.5 %all-to-all-start.1 = ((bf16[4,3,256,384]{3,2,1,0:T(8,128)(2,1)}), bf16[4,3,256,384]{3,2,1,0:T(8,128)(2,1)}, u32[]{:S(2)}, u32[]{:S(2)}) async-start(bf16[4,3,256,384]{3,2,1,0:T(8,128)(2,1)} %bitcast.66), calls=%async_computation.1 | async-start | bytes 4718592 | tf_op jit(solution)/shard_map/cond/branch_1_fun/all_to_all | solution.py:110
  77.9 2.0 collective-permute-start.6
  81.4 14.9 %collective-permute-done.5 = bf16[2,272,1024]{2,1,0:T(8,128)(2,1)} collective-permute-done((bf16[2,272,1024]{2,1,0:T(8,128)(2,1)S(1)}, bf16[2,272,1024]{2,1,0:T(8,128)(2,1)}, u32[]{:S(2)}, u32[]{:S(2)}) %collective-permute-start.5) | collective-permute-done | bytes 1114144 | tf_op jit(solution)/shard_map/cond/branch_1_fun/ppermute | solution.py:20
  97.7 23.9 %all-to-all-done.1.pool = bf16[4,3,256,384]{3,2,1,0:T(8,128)(2,1)} async-done(((bf16[4,3,256,384]{3,2,1,0:T(8,128)(2,1)}), bf16[4,3,256,384]{3,2,1,0:T(8,128)(2,1)}, u32[]{:S(2)}, u32[]{:S(2)}) %all-to-all-start.1) | async-done | bytes 2359328 | tf_op jit(solution)/shard_map/cond/branch_1_fun/all_to_all | solution.py:110
  121.6 4.8 %branch_1_fun.10 = (bf16[3,3,256,384]{3,2,1,0:T(8,128)(2,1)}, bf16[1,3,256,384]{3,2,1,0:T(8,128)(2,1)}) custom-call(s32[17]{0:T(128)} %get-tuple-element.130.facts, bf16[4,3,256,384]{3,2,1,0:T(8,128)(2,1)} %all-to-all-done.1.pool), custom_call_target="tpu_custom_call" | custom-call | bytes 4718592 | tf_op jit(solution)/shard_map/cond/branch_1_fun/pallas_call | solution.py:127
  126.3 4.6 %collective-permute-done.6 = bf16[2,272,1024]{2,1,0:T(8,128)(2,1)} collective-permute-done((bf16[2,272,1024]{2,1,0:T(8,128)(2,1)S(1)}, bf16[2,272,1024]{2,1,0:T(8,128)(2,1)}, u32[]{:S(2)}, u32[]{:S(2)}) %collective-permute-start.6) | collective-permute-done | bytes 1114144 | tf_op jit(solution)/shard_map/cond/branch_1_fun/ppermute | solution.py:20
  131.0 12.9 %collective-permute-done.4 = bf16[2,272,1024]{2,1,0:T(8,128)(2,1)} collective-permute-done((bf16[2,272,1024]{2,1,0:T(8,128)(2,1)}, bf16[2,272,1024]{2,1,0:T(8,128)(2,1)}, u32[]{:S(2)}, u32[]{:S(2)}) %collective-permute-start.4) | collective-permute-done | bytes 1114144 | tf_op jit(solution)/shard_map/cond/branch_1_fun/ppermute | solution.py:20
  143.9 9.4 %collective-permute-done.7 = bf16[2,272,1024]{2,1,0:T(8,128)(2,1)} collective-permute-done((bf16[2,272,1024]{2,1,0:T(8,128)(2,1)}, bf16[2,272,1024]{2,1,0:T(8,128)(2,1)}, u32[]{:S(2)}, u32[]{:S(2)}) %collective-permute-start.7) | collective-permute-done | bytes 1114144 | tf_op jit(solution)/shard_map/cond/branch_1_fun/ppermute | solution.py:20
  153.3 2.5 collective-permute-start.26
  157.3 38.2 %conditional.14 = (bf16[3,1024,384]{2,1,0:T(8,128)(2,1)S(1)}, bf16[2048,1024]{1,0:T(8,128)(2,1)}, bf16[2048,1024]{1,0:T(8,128)(2,1)}, f32[2048,1]{0,1:T(1,128)S(1)}, bf16[4,3,256,384]{3,2,0,1:T(8,128)(2,1)}) conditional(s32[]{:T(128)} %bitcast.24, () %tuple.98, (s32[17]{0:T(128)}, bf16[4,3,256,384]{3,2,1,0:T(8,128)(2,1)}, ...), branch_computations={%region_13.14_spmd, %region_14.16_spmd} | conditional | flops 6301699 | bytes 72184032 | solution.py:381
  157.3 4.8 %branch_1_fun.11 = bf16[4,3,256,384]{3,2,1,0:T(8,128)(2,1)} custom-call(s32[17]{0:T(128)} %get-tuple-element.133.facts, bf16[4,3,256,384]{3,2,1,0:T(8,128)(2,1)} %get-tuple-element.134.pool, bf16[3,3,256,384]{3,2,1,0:T(8,128)(2,1)} %get-tuple-element.135.came, bf16[1,3,256,384]{3,2,1,0:T(8,128)(2,1)S(1)} %get-tuple-element.136.fourth), custom_call_target="tpu_custom_call" | custom-call | bytes 7077888 | tf_op jit(solution)/shard_map/cond/branch_1_fun/pallas_call | solution.py:182
  162.1 3.6 all-to-all-start.2
  168.2 5.5 %branch_1_fun.12 = (bf16[16,128,1024]{2,1,0:T(8,128)(2,1)}, bf16[16,128,1024]{2,1,0:T(8,128)(2,1)S(1)}, bf16[16,16,1024]{2,1,0:T(8,128)(2,1)S(1)}) custom-call(bf16[2,272,1024]{2,1,0:T(8,128)(2,1)} %get-tuple-element.137.refs_0_, bf16[2,272,1024]{2,1,0:T(8,128)(2,1)S(1)} %get-tuple-element.138.refs_1_, bf16[2,272,1024]{2,1,0:T(8,128)(2,1)} %get-tuple-element.139.refs_2_, ...), custom_call_target="tpu_custom_call" | custom-call | bytes 17825792 | tf_op jit(solution)/shard_map/cond/branch_1_fun/pallas_call | solution.py:221
  173.8 2.1 copy-done.1
  176.9 5.0 %fusion = bf16[2048,1024]{1,0:T(8,128)(2,1)} fusion(bf16[16,128,1024]{2,1,0:T(8,128)(2,1)} %copy-done.1, f32[2048]{0:T(1024)S(1)} %bitcast.72), kind=kLoop, calls=%fused_computation.4 | loop fusion | flops 6291456 | bytes 8396800 | tf_op jit(solution)/shard_map/cond/branch_1_fun/convert_element_type | solution.py:442
  181.8 10.3 %all-to-all-done.2 = bf16[4,3,256,384]{3,2,1,0:T(8,128)(2,1)S(1)} async-done(((bf16[4,3,256,384]{3,2,1,0:T(8,128)(2,1)}), bf16[4,3,256,384]{3,2,1,0:T(8,128)(2,1)S(1)}, u32[]{:S(2)}, u32[]{:S(2)}) %all-to-all-start.2) | async-done | bytes 2359328 | tf_op jit(solution)/shard_map/cond/branch_1_fun/all_to_all | solution.py:320
  193.5 1.9 copy.30
  195.5 36.5 %conditional.15 = (bf16[2048,384]{1,0:T(8,128)(2,1)}, bf16[2048,384]{1,0:T(8,128)(2,1)}, bf16[2048,384]{1,0:T(8,128)(2,1)}, bf16[2048,512]{1,0:T(8,128)(2,1)}, b...) conditional(s32[]{:T(128)} %bitcast.24, () %tuple.97, (s32[2,16]{1,0:T(2,128)S(1)}, ...), branch_computations={%region_16.17_spmd, %region_17.20_spmd} | conditional | flops 6442450944 | bytes 74727584 | solution.py:381
  195.5 3.3 copy.34
  198.8 4.5 %all-to-all-start = ((bf16[4,3,256,384]{3,2,1,0:T(8,128)(2,1)}), bf16[4,3,256,384]{3,2,1,0:T(8,128)(2,1)}, u32[]{:S(2)}, u32[]{:S(2)}) async-start(bf16[4,3,256,384]{3,2,1,0:T(8,128)(2,1)} %copy.34), calls=%async_computation | async-start | bytes 4718592 | tf_op jit(solution)/shard_map/cond/branch_1_fun/all_to_all | solution.py:110
  204.8 10.1 %branch_1_fun.13 = bf16[3,2048,384]{2,1,0:T(8,128)(2,1)S(1)} custom-call(bf16[2048,1024]{1,0:T(8,128)(2,1)} %get-tuple-element.150.x_rows, bf16[2048,1024]{1,0:T(8,128)(2,1)} %get-tuple-element.151.dy_rows, bf16[3,1024,384]{2,1,0:T(8,128)(2,1)S(1)} %get-tuple-element.152.weight.refs_3_), custom_call_target="tpu_custom_call" | custom-call | flops 4831838208 | bytes 15466496 | tf_op jit(solution)/shard_map/cond/branch_1_fun/pallas_call | solution.py:247
  214.9 8.1 %conditional = (bf16[3,2048,384]{2,1,0:T(8,128)(2,1)S(1)}, bf16[3,2048,384]{2,1,0:T(8,128)(2,1)}) conditional(s32[]{:T(128)} %bitcast.19, () %tuple.66, bf16[3,2048,384]{2,1,0:T(8,128)(2,1)S(1)} %branch_1_fun.13), branch_computations={%region_18.18_spmd, %region_19.19_spmd} | conditional | bytes 28311608 | solution.py:381
  215.5 7.5 %collective-permute-done.1 = bf16[3,2048,384]{2,1,0:T(8,128)(2,1)} collective-permute-done((bf16[3,2048,384]{2,1,0:T(8,128)(2,1)S(1)}, bf16[3,2048,384]{2,1,0:T(8,128)(2,1)}, u32[]{:S(2)}, u32[]{:S(2)}) %collective-permute-start.1) | collective-permute-done | bytes 4718624 | tf_op jit(solution)/shard_map/cond/branch_1_fun/cond/branch_1_fun/ppermute | solution.py:30
  223.1 8.8 %branch_1_fun.14 = (bf16[2048,384]{1,0:T(8,128)(2,1)}, bf16[2048,384]{1,0:T(8,128)(2,1)}, bf16[2048,384]{1,0:T(8,128)(2,1)}, bf16[2048,512]{1,0:T(8,128)(2,1)}, bf16[2048,512]{1,0:T(8,128)(2,1)}) custom-call(bf16[3,2048,384]{2,1,0:T(8,128)(2,1)S(1)} %get-tuple-element.153.refs_0_, bf16[3,2048,384]{2,1,0:T(8,128)(2,1)} %get-tuple-element.154.refs_1_, ...), custom_call_target="tpu_custom_call" | custom-call | flops 1610612736 | bytes 19136512 | tf_op jit(solution)/shard_map/cond/branch_1_fun/pallas_call | solution.py:299
  232.0 4.6 %conditional.17 = ((bf16[3,3,256,384]{3,2,1,0:T(8,128)(2,1)}, bf16[1,3,256,384]{3,2,1,0:T(8,128)(2,1)S(1)})) conditional(s32[]{:T(128)} %bitcast.24, () %tuple.108, (s32[17]{0:T(128)}, bf16[4,3,256,384]{3,2,1,0:T(8,128)(2,1)}) %tuple.109), branch_computations={%region_22.23_spmd, %region_23.24_spmd} | conditional | bytes 4718600 | solution.py:381
  232.0 4.6 %branch_1_fun.15 = (bf16[3,3,256,384]{3,2,1,0:T(8,128)(2,1)}, bf16[1,3,256,384]{3,2,1,0:T(8,128)(2,1)S(1)}) custom-call(s32[17]{0:T(128)} %get-tuple-element.162.facts, bf16[4,3,256,384]{3,2,1,0:T(8,128)(2,1)} %get-tuple-element.163.pool), custom_call_target="tpu_custom_call" | custom-call | bytes 4718592 | tf_op jit(solution)/shard_map/cond/branch_1_fun/pallas_call | solution.py:127
  237.1 80.6 %conditional.18 = (bf16[512,1024]{1,0:T(8,128)(2,1)}, bf16[512,1024]{0,1:T(8,128)(2,1)}, f32[1024,384]{1,0:T(8,128)}, f32[1024,384]{1,0:T(8,128)}, f32[1024,384]...) conditional(s32[]{:T(128)} %bitcast.24, () %tuple.96, (bf16[2048,512]{1,0:T(8,128)(2,1)}, ...), branch_computations={%region_26.27_spmd, %region_27.28_spmd} | conditional | flops 8071938048 | bytes 110362992 | solution.py:381
  238.4 2.0 collective-permute-start.17
  241.7 1.5 collective-permute-start.18
  243.2 2.7 fusion.5
  245.9 2.7 fusion.2
  248.6 2.7 add_convert_fusion.1
  251.4 2.7 add_convert_fusion
  254.2 6.2 %fusion.16 = f32[1024,384]{1,0:T(8,128)} fusion(bf16[2048,1024]{1,0:T(8,128)(2,1)} %get-tuple-element.173, bf16[2048,384]{1,0:T(8,128)(2,1)} %get-tuple-element.165), kind=kOutput, calls=%fused_computation.67 | convolution fusion | flops 1610612736 | bytes 7340032 | tf_op jit(solution)/shard_map/cond/branch_1_fun/dot_general | solution.py:350
  260.4 6.3 %fusion.17 = f32[1024,384]{1,0:T(8,128)} fusion(bf16[2048,1024]{1,0:T(8,128)(2,1)} %get-tuple-element.173, bf16[2048,384]{1,0:T(8,128)(2,1)} %get-tuple-element.167), kind=kOutput, calls=%fused_computation.68 | convolution fusion | flops 1610612736 | bytes 7340032 | tf_op jit(solution)/shard_map/cond/branch_1_fun/dot_general | solution.py:350
  270.5 6.2 %fusion.18 = f32[1024,384]{1,0:T(8,128)} fusion(bf16[2048,1024]{1,0:T(8,128)(2,1)} %get-tuple-element.174, bf16[2048,384]{1,0:T(8,128)(2,1)} %get-tuple-element.175), kind=kOutput, calls=%fused_computation.69 | convolution fusion | flops 1610612736 | bytes 7340032 | tf_op jit(solution)/shard_map/cond/branch_1_fun/dot_general | solution.py:350
  276.7 5.0 %branch_1_fun.16 = bf16[4,3,256,384]{3,2,1,0:T(8,128)(2,1)} custom-call(s32[17]{0:T(128)} %get-tuple-element.176.facts, bf16[4,3,256,384]{3,2,1,0:T(8,128)(2,1)} %get-tuple-element.177.pool, bf16[3,3,256,384]{3,2,1,0:T(8,128)(2,1)} %get-tuple-element.178.came, bf16[1,3,256,384]{3,2,1,0:T(8,128)(2,1)} %get-tuple-element.179.fourth), custom_call_target="tpu_custom_call" | custom-call | bytes 7077888 | tf_op jit(solution)/shard_map/cond/branch_1_fun/pallas_call | solution.py:182
  284.4 18.2 %collective-permute-done.19 = bf16[512,512]{1,0:T(8,128)(2,1)S(1)} collective-permute-done((bf16[512,512]{1,0:T(8,128)(2,1)S(1)}, bf16[512,512]{1,0:T(8,128)(2,1)S(1)}, u32[]{:S(2)}, u32[]{:S(2)}) %collective-permute-start.19) | collective-permute-done | bytes 524320 | tf_op jit(solution)/shard_map/cond/branch_1_fun/ppermute | solution.py:20
  304.9 1.5 collective-permute-start.24
  308.8 7.3 %collective-permute-done.22 = bf16[512,512]{0,1:T(8,128)(2,1)S(1)} collective-permute-done((bf16[512,512]{0,1:T(8,128)(2,1)S(1)}, bf16[512,512]{0,1:T(8,128)(2,1)S(1)}, u32[]{:S(2)}, u32[]{:S(2)}) %collective-permute-start.22) | collective-permute-done | bytes 524320 | tf_op jit(solution)/shard_map/cond/branch_1_fun/ppermute | solution.py:20
  317.7 63.4 %conditional.20 = (bf16[128,1024]{1,0:T(8,128)(2,1)}, bf16[128,1024]{1,0:T(8,128)(2,1)}, bf16[4,6,256,384]{3,2,1,0:T(8,128)(2,1)}) conditional(s32[]{:T(128)} %bitcast.24, () %tuple.95, (bf16[512,1024]{1,0:T(8,128)(2,1)}, bf16[512,1024]{0,1:T(8,128)(2,1)}, s32[17]{0:T(128)}, bf16[4,3,256,384]{3,2,1,0:T(8,128)(2,1)}, ...), branch_computations={%region_28.29_spmd, %region_29.30_spmd} | conditional | flops 3145728 | bytes 61079796 | solution.py:381
  317.7 4.3 %branch_1_fun.17 = bf16[4,6,256,384]{3,2,1,0:T(8,128)(2,1)S(1)} custom-call(s32[17]{0:T(128)} %get-tuple-element.182.facts, bf16[4,3,256,384]{3,2,1,0:T(8,128)(2,1)} %get-tuple-element.183.pool, bf16[3,3,256,384]{3,2,1,0:T(8,128)(2,1)} %get-tuple-element.184.came, bf16[1,3,256,384]{3,2,1,0:T(8,128)(2,1)S(1)} %get-tuple-element.185.fourth, ...), custom_call_target="tpu_custom_call" | custom-call | bytes 11796480 | tf_op jit(solution)/shard_map/cond/branch_1_fun/pallas_call | solution.py:182
  322.0 2.1 copy-done
  324.1 5.0 %all-to-all-start.3 = ((bf16[4,6,256,384]{3,2,1,0:T(8,128)(2,1)}), bf16[4,6,256,384]{3,2,1,0:T(8,128)(2,1)}, u32[]{:S(2)}, u32[]{:S(2)}) async-start(bf16[4,6,256,384]{3,2,1,0:T(8,128)(2,1)} %copy-done), calls=%async_computation.3 | async-start | bytes 9437184 | tf_op jit(solution)/shard_map/cond/branch_1_fun/all_to_all | solution.py:489
  331.8 2.1 collective-permute-start.8
  333.9 14.5 %collective-permute-done.10 = bf16[256,1024]{1,0:T(8,128)(2,1)S(1)} collective-permute-done((bf16[256,1024]{1,0:T(8,128)(2,1)S(1)}, bf16[256,1024]{1,0:T(8,128)(2,1)S(1)}, u32[]{:S(2)}, u32[]{:S(2)}) %collective-permute-start.10) | collective-permute-done | bytes 524320 | tf_op jit(solution)/shard_map/cond/branch_1_fun/ppermute | solution.py:20
  348.8 10.9 %collective-permute-done.8 = bf16[256,1024]{1,0:T(8,128)(2,1)S(1)} collective-permute-done((bf16[256,1024]{1,0:T(8,128)(2,1)S(1)}, bf16[256,1024]{1,0:T(8,128)(2,1)S(1)}, u32[]{:S(2)}, u32[]{:S(2)}) %collective-permute-start.8) | collective-permute-done | bytes 524320 | tf_op jit(solution)/shard_map/cond/branch_1_fun/ppermute | solution.py:20
  361.0 2.2 collective-permute-done.11
  364.0 7.7 %collective-permute-done.9 = bf16[128,1024]{1,0:T(8,128)(2,1)S(1)} collective-permute-done((bf16[128,1024]{1,0:T(8,128)(2,1)S(1)}, bf16[128,1024]{1,0:T(8,128)(2,1)S(1)}, u32[]{:S(2)}, u32[]{:S(2)}) %collective-permute-start.9) | collective-permute-done | bytes 262176 | tf_op jit(solution)/shard_map/cond/branch_1_fun/ppermute | solution.py:20
  372.5 8.7 %all-to-all-done.3 = bf16[4,6,256,384]{3,2,1,0:T(8,128)(2,1)} async-done(((bf16[4,6,256,384]{3,2,1,0:T(8,128)(2,1)}), bf16[4,6,256,384]{3,2,1,0:T(8,128)(2,1)}, u32[]{:S(2)}, u32[]{:S(2)}) %all-to-all-start.3) | async-done | bytes 4718624 | tf_op jit(solution)/shard_map/cond/branch_1_fun/all_to_all | solution.py:489
  381.1 9.9 %shard_map.132 = (bf16[1,3,1024,384]{3,2,1,0:T(8,128)(2,1)}, bf16[1,3,1024,384]{3,2,1,0:T(8,128)(2,1)}, bf16[1,3,1024,384]{3,2,1,0:T(8,128)(2,1)}) custom-call(bf16[3,1024,384]{2,1,0:T(8,128)(2,1)S(1)} %get-tuple-element.262.weight, bf16[4,6,256,384]{3,2,1,0:T(8,128)(2,1)} %get-tuple-element.287.moments, f32[1024,384]{1,0:T(8,128)} %get-tuple-element.288.grad_gate, ...), custom_call_target="tpu_custom_call" | custom-call | flops 47185920 | bytes 18874368 | tf_op jit(solution)/shard_map/pallas_call | solution.py:53
  (114 shorter events, 40.0 us)
Async XLA Ops:
  0.6 0.7 copy-start.12
  0.6 0.7 copy-start.11
  0.7 0.8 copy-start.10
  0.7 2.0 copy-start.7
  0.7 2.0 copy-start.6
  0.7 2.0 copy-start.2
  2.7 28.8 %collective-permute-start.12 = (bf16[1,272,1024]{2,1,0:T(8,128)(2,1)S(1)}, bf16[1,272,1024]{2,1,0:T(8,128)(2,1)S(1)}, u32[]{:S(2)}, u32[]{:S(2)}) collective-permute-start(bf16[1,272,1024]{2,1,0:T(8,128)(2,1)S(1)} %bitcast.69), channel_id=1, source_target_pairs={{0,16},{2,18},{4,20},{6,22},{8,24},{10,26},{12,28},{14,30},{16,0},... | collective-permute-start | bytes 1671176 | tf_op jit(solution)/shard_map/cond/branch_1_fun/ppermute | solution.py:20
  6.8 31.6 %collective-permute-start.13 = (bf16[1,272,1024]{2,1,0:T(8,128)(2,1)S(1)}, bf16[1,272,1024]{2,1,0:T(8,128)(2,1)S(1)}, u32[]{:S(2)}, u32[]{:S(2)}) collective-permute-start(bf16[1,272,1024]{2,1,0:T(8,128)(2,1)S(1)} %bitcast.70), channel_id=1, source_target_pairs={{0,8},{2,10},{4,12},{6,14},{8,0},{10,2},{12,4},{14,6},{16,24},{18,... | collective-permute-start | bytes 1671176 | tf_op jit(solution)/shard_map/cond/branch_1_fun/ppermute | solution.py:20
  11.7 36.9 %all-to-all-start.4 = ((bf16[4,3,256,384]{3,2,1,0:T(8,128)(2,1)}), bf16[4,3,256,384]{3,2,1,0:T(8,128)(2,1)}, u32[]{:S(2)}, u32[]{:S(2)}) async-start(bf16[4,3,256,384]{3,2,1,0:T(8,128)(2,1)} %bitcast.63), calls=%async_computation.4 | async-start | bytes 4718592 | tf_op jit(solution)/shard_map/cond/branch_1_fun/all_to_all | solution.py:110
  32.6 35.0 %collective-permute-start.15 = (bf16[2,272,1024]{2,1,0:T(8,128)(2,1)}, bf16[2,272,1024]{2,1,0:T(8,128)(2,1)}, u32[]{:S(2)}, u32[]{:S(2)}) collective-permute-start(bf16[2,272,1024]{2,1,0:T(8,128)(2,1)} %pad_maximum_fusion.2), channel_id=1, source_target_pairs={{0,2},{2,0},{4,6},{6,4},{8,10},{10,8},{12,14},{14,12},{16,18},{18,... | collective-permute-start | bytes 3342344 | tf_op jit(solution)/shard_map/cond/branch_1_fun/ppermute | solution.py:20
  34.1 33.4 %collective-permute-start.16 = (bf16[2,272,1024]{2,1,0:T(8,128)(2,1)}, bf16[2,272,1024]{2,1,0:T(8,128)(2,1)}, u32[]{:S(2)}, u32[]{:S(2)}) collective-permute-start(bf16[2,272,1024]{2,1,0:T(8,128)(2,1)} %pad_maximum_fusion.2), channel_id=1, source_target_pairs={{0,4},{2,6},{4,0},{6,2},{8,12},{10,14},{12,8},{14,10},{16,20},{18,... | collective-permute-start | bytes 3342344 | tf_op jit(solution)/shard_map/cond/branch_1_fun/ppermute | solution.py:20
  35.7 12.9 %collective-permute-start.14 = (bf16[1,272,1024]{2,1,0:T(8,128)(2,1)S(1)}, bf16[1,272,1024]{2,1,0:T(8,128)(2,1)S(1)}, u32[]{:S(2)}, u32[]{:S(2)}) collective-permute-start(bf16[1,272,1024]{2,1,0:T(8,128)(2,1)S(1)} %collective-permute-done.12), channel_id=1, source_target_pairs={{0,8},{2,10},{4,12},{6,14},{8,0},{10,2},{12,4},{14,6},{16,24},{18,... | collective-permute-start | bytes 1671176 | tf_op jit(solution)/shard_map/cond/branch_1_fun/ppermute | solution.py:20
  68.2 85.1 %collective-permute-start.25 = (bf16[3,3,256,384]{3,2,1,0:T(8,128)(2,1)}, bf16[3,3,256,384]{3,2,1,0:T(8,128)(2,1)}, u32[]{:S(2)}, u32[]{:S(2)}) collective-permute-start(bf16[3,3,256,384]{3,2,1,0:T(8,128)(2,1)} %get-tuple-element.245), channel_id=1, source_target_pairs={{0,16},{2,18},{4,20},{6,22},{8,24},{10,26},{12,28},{14,30},{16,0},... | collective-permute-start | bytes 5308424 | tf_op jit(solution)/shard_map/ppermute | solution.py:20
  68.6 87.2 %copy-start.3 = (bf16[1,3,1024,384]{3,2,1,0:T(8,128)(2,1)S(1)}, bf16[1,3,1024,384]{3,2,1,0:T(8,128)(2,1)}, u32[]{:S(2)}) copy-start(bf16[1,3,1024,384]{3,2,1,0:T(8,128)(2,1)} %param.39) | copy-start | bytes 7077892
  68.6 27.6 %collective-permute-start.5 = (bf16[2,272,1024]{2,1,0:T(8,128)(2,1)S(1)}, bf16[2,272,1024]{2,1,0:T(8,128)(2,1)}, u32[]{:S(2)}, u32[]{:S(2)}) collective-permute-start(bf16[2,272,1024]{2,1,0:T(8,128)(2,1)S(1)} %get-tuple-element.128), channel_id=1, source_target_pairs={{0,2},{2,0},{4,6},{6,4},{8,10},{10,8},{12,14},{14,12},{16,18},{18,... | collective-permute-start | bytes 3342344 | tf_op jit(solution)/shard_map/cond/branch_1_fun/ppermute | solution.py:20
  73.4 48.2 %all-to-all-start.1 = ((bf16[4,3,256,384]{3,2,1,0:T(8,128)(2,1)}), bf16[4,3,256,384]{3,2,1,0:T(8,128)(2,1)}, u32[]{:S(2)}, u32[]{:S(2)}) async-start(bf16[4,3,256,384]{3,2,1,0:T(8,128)(2,1)} %bitcast.66), calls=%async_computation.1 | async-start | bytes 4718592 | tf_op jit(solution)/shard_map/cond/branch_1_fun/all_to_all | solution.py:110
  77.9 53.0 %collective-permute-start.6 = (bf16[2,272,1024]{2,1,0:T(8,128)(2,1)S(1)}, bf16[2,272,1024]{2,1,0:T(8,128)(2,1)}, u32[]{:S(2)}, u32[]{:S(2)}) collective-permute-start(bf16[2,272,1024]{2,1,0:T(8,128)(2,1)S(1)} %get-tuple-element.128), channel_id=1, source_target_pairs={{0,4},{2,6},{4,0},{6,2},{8,12},{10,14},{12,8},{14,10},{16,20},{18,... | collective-permute-start | bytes 3342344 | tf_op jit(solution)/shard_map/cond/branch_1_fun/ppermute | solution.py:20
  79.9 64.0 %collective-permute-start.4 = (bf16[2,272,1024]{2,1,0:T(8,128)(2,1)}, bf16[2,272,1024]{2,1,0:T(8,128)(2,1)}, u32[]{:S(2)}, u32[]{:S(2)}) collective-permute-start(bf16[2,272,1024]{2,1,0:T(8,128)(2,1)} %get-tuple-element.127), channel_id=1, source_target_pairs={{0,2},{2,0},{4,6},{6,4},{8,10},{10,8},{12,14},{14,12},{16,18},{18,... | collective-permute-start | bytes 3342344 | tf_op jit(solution)/shard_map/cond/branch_1_fun/ppermute | solution.py:20
  96.3 57.0 %collective-permute-start.7 = (bf16[2,272,1024]{2,1,0:T(8,128)(2,1)}, bf16[2,272,1024]{2,1,0:T(8,128)(2,1)}, u32[]{:S(2)}, u32[]{:S(2)}) collective-permute-start(bf16[2,272,1024]{2,1,0:T(8,128)(2,1)} %collective-permute-done.5), channel_id=1, source_target_pairs={{0,4},{2,6},{4,0},{6,2},{8,12},{10,14},{12,8},{14,10},{16,20},{18,... | collective-permute-start | bytes 3342344 | tf_op jit(solution)/shard_map/cond/branch_1_fun/ppermute | solution.py:20
  153.3 83.3 %collective-permute-start.26 = (bf16[3,3,256,384]{3,2,1,0:T(8,128)(2,1)}, bf16[3,3,256,384]{3,2,1,0:T(8,128)(2,1)}, u32[]{:S(2)}, u32[]{:S(2)}) collective-permute-start(bf16[3,3,256,384]{3,2,1,0:T(8,128)(2,1)} %get-tuple-element.271), channel_id=1, source_target_pairs={{0,16},{2,18},{4,20},{6,22},{8,24},{10,26},{12,28},{14,30},{16,0},... | collective-permute-start | bytes 5308424 | tf_op jit(solution)/shard_map/ppermute | solution.py:20
  155.8 1.5 copy-start.5
  162.1 30.0 %all-to-all-start.2 = ((bf16[4,3,256,384]{3,2,1,0:T(8,128)(2,1)}), bf16[4,3,256,384]{3,2,1,0:T(8,128)(2,1)S(1)}, u32[]{:S(2)}, u32[]{:S(2)}) async-start(bf16[4,3,256,384]{3,2,1,0:T(8,128)(2,1)} %branch_1_fun.11), calls=%async_computation.2 | async-start | bytes 4718592 | tf_op jit(solution)/shard_map/cond/branch_1_fun/all_to_all | solution.py:320
  173.8 2.1 copy-start.1
  176.9 5.0 %copy-start.8 = (f32[16,128]{1,0:T(8,128)}, f32[16,128]{1,0:T(8,128)S(1)}, u32[]{:S(2)}) copy-start(f32[16,128]{1,0:T(8,128)S(1)} %convert_reduce_fusion) | copy-start | bytes 24580 | tf_op jit(solution)/shard_map/cond
  192.1 1.4 copy-start.4
  193.5 2.0 copy-start.9
  198.8 33.1 %all-to-all-start = ((bf16[4,3,256,384]{3,2,1,0:T(8,128)(2,1)}), bf16[4,3,256,384]{3,2,1,0:T(8,128)(2,1)}, u32[]{:S(2)}, u32[]{:S(2)}) async-start(bf16[4,3,256,384]{3,2,1,0:T(8,128)(2,1)} %copy.34), calls=%async_computation | async-start | bytes 4718592 | tf_op jit(solution)/shard_map/cond/branch_1_fun/all_to_all | solution.py:110
  214.9 8.1 %collective-permute-start.1 = (bf16[3,2048,384]{2,1,0:T(8,128)(2,1)S(1)}, bf16[3,2048,384]{2,1,0:T(8,128)(2,1)}, u32[]{:S(2)}, u32[]{:S(2)}) collective-permute-start(bf16[3,2048,384]{2,1,0:T(8,128)(2,1)S(1)} %param.10), channel_id=1, source_target_pairs={{0,1},{1,0},{2,3},{3,2},{4,5},{5,4},{6,7},{7,6},{8,9},{9,8},{10,11... | collective-permute-start | bytes 14155784 | tf_op jit(solution)/shard_map/cond/branch_1_fun/cond/branch_1_fun/ppermute | solution.py:30
  236.6 81.0 %collective-permute-start.27 = (bf16[3,3,256,384]{3,2,1,0:T(8,128)(2,1)}, bf16[3,3,256,384]{3,2,1,0:T(8,128)(2,1)}, u32[]{:S(2)}, u32[]{:S(2)}) collective-permute-start(bf16[3,3,256,384]{3,2,1,0:T(8,128)(2,1)} %get-tuple-element.280), channel_id=1, source_target_pairs={{0,16},{2,18},{4,20},{6,22},{8,24},{10,26},{12,28},{14,30},{16,0},... | collective-permute-start | bytes 5308424 | tf_op jit(solution)/shard_map/ppermute | solution.py:20
  238.4 28.3 %collective-permute-start.17 = (bf16[1024,512]{1,0:T(8,128)(2,1)S(1)}, bf16[1024,512]{1,0:T(8,128)(2,1)S(1)}, u32[]{:S(2)}, u32[]{:S(2)}) collective-permute-start(bf16[1024,512]{1,0:T(8,128)(2,1)S(1)} %slice.101), channel_id=1, source_target_pairs={{0,2},{2,0},{4,6},{6,4},{8,10},{10,8},{12,14},{14,12},{16,18},{18,... | collective-permute-start | bytes 3145736 | tf_op jit(solution)/shard_map/cond/branch_1_fun/ppermute | solution.py:20
  241.7 25.0 %collective-permute-start.18 = (bf16[1024,512]{1,0:T(8,128)(2,1)S(1)}, bf16[1024,512]{1,0:T(8,128)(2,1)S(1)}, u32[]{:S(2)}, u32[]{:S(2)}) collective-permute-start(bf16[1024,512]{1,0:T(8,128)(2,1)S(1)} %slice.102), channel_id=1, source_target_pairs={{0,4},{2,6},{4,0},{6,2},{8,12},{10,14},{12,8},{14,10},{16,20},{18,... | collective-permute-start | bytes 3145736 | tf_op jit(solution)/shard_map/cond/branch_1_fun/ppermute | solution.py:20
  266.7 37.1 %collective-permute-start.21 = (bf16[1024,512]{0,1:T(8,128)(2,1)S(1)}, bf16[1024,512]{0,1:T(8,128)(2,1)S(1)}, u32[]{:S(2)}, u32[]{:S(2)}) collective-permute-start(bf16[1024,512]{0,1:T(8,128)(2,1)S(1)} %slice.132), channel_id=1, source_target_pairs={{0,2},{2,0},{4,6},{6,4},{8,10},{10,8},{12,14},{14,12},{16,18},{18,... | collective-permute-start | bytes 3145736 | tf_op jit(solution)/shard_map/cond/branch_1_fun/ppermute | solution.py:20
  267.2 37.5 %collective-permute-start.23 = (bf16[1024,512]{0,1:T(8,128)(2,1)S(1)}, bf16[1024,512]{0,1:T(8,128)(2,1)S(1)}, u32[]{:S(2)}, u32[]{:S(2)}) collective-permute-start(bf16[1024,512]{0,1:T(8,128)(2,1)S(1)} %slice.133), channel_id=1, source_target_pairs={{0,4},{2,6},{4,0},{6,2},{8,12},{10,14},{12,8},{14,10},{16,20},{18,... | collective-permute-start | bytes 3145736 | tf_op jit(solution)/shard_map/cond/branch_1_fun/ppermute | solution.py:20
  269.6 33.0 %collective-permute-start.19 = (bf16[512,512]{1,0:T(8,128)(2,1)S(1)}, bf16[512,512]{1,0:T(8,128)(2,1)S(1)}, u32[]{:S(2)}, u32[]{:S(2)}) collective-permute-start(bf16[512,512]{1,0:T(8,128)(2,1)S(1)} %add_convert_fusion.9), channel_id=1, source_target_pairs={{0,4},{2,6},{4,0},{6,2},{8,12},{10,14},{12,8},{14,10},{16,20},{18,... | collective-permute-start | bytes 1572872 | tf_op jit(solution)/shard_map/cond/branch_1_fun/ppermute | solution.py:20
  282.9 23.6 %collective-permute-start.20 = (bf16[512,512]{1,0:T(8,128)(2,1)S(1)}, bf16[512,512]{1,0:T(8,128)(2,1)S(1)}, u32[]{:S(2)}, u32[]{:S(2)}) collective-permute-start(bf16[512,512]{1,0:T(8,128)(2,1)S(1)} %add_convert_fusion.7), channel_id=1, source_target_pairs={{0,2},{2,0},{4,6},{6,4},{8,10},{10,8},{12,14},{14,12},{16,18},{18,... | collective-permute-start | bytes 1572872 | tf_op jit(solution)/shard_map/cond/branch_1_fun/ppermute | solution.py:20
  304.0 12.1 %collective-permute-start.22 = (bf16[512,512]{0,1:T(8,128)(2,1)S(1)}, bf16[512,512]{0,1:T(8,128)(2,1)S(1)}, u32[]{:S(2)}, u32[]{:S(2)}) collective-permute-start(bf16[512,512]{0,1:T(8,128)(2,1)S(1)} %add_convert_fusion.5), channel_id=1, source_target_pairs={{0,4},{2,6},{4,0},{6,2},{8,12},{10,14},{12,8},{14,10},{16,20},{18,... | collective-permute-start | bytes 1572872 | tf_op jit(solution)/shard_map/cond/branch_1_fun/ppermute | solution.py:20
  304.9 11.5 %collective-permute-start.24 = (bf16[512,512]{0,1:T(8,128)(2,1)S(1)}, bf16[512,512]{0,1:T(8,128)(2,1)S(1)}, u32[]{:S(2)}, u32[]{:S(2)}) collective-permute-start(bf16[512,512]{0,1:T(8,128)(2,1)S(1)} %add_convert_fusion.3), channel_id=1, source_target_pairs={{0,2},{2,0},{4,6},{6,4},{8,10},{10,8},{12,14},{14,12},{16,18},{18,... | collective-permute-start | bytes 1572872 | tf_op jit(solution)/shard_map/cond/branch_1_fun/ppermute | solution.py:20
  322.0 2.2 copy-start
  324.1 57.0 %all-to-all-start.3 = ((bf16[4,6,256,384]{3,2,1,0:T(8,128)(2,1)}), bf16[4,6,256,384]{3,2,1,0:T(8,128)(2,1)}, u32[]{:S(2)}, u32[]{:S(2)}) async-start(bf16[4,6,256,384]{3,2,1,0:T(8,128)(2,1)} %copy-done), calls=%async_computation.3 | async-start | bytes 9437184 | tf_op jit(solution)/shard_map/cond/branch_1_fun/all_to_all | solution.py:489
  330.6 17.7 %collective-permute-start.10 = (bf16[256,1024]{1,0:T(8,128)(2,1)S(1)}, bf16[256,1024]{1,0:T(8,128)(2,1)S(1)}, u32[]{:S(2)}, u32[]{:S(2)}) collective-permute-start(bf16[256,1024]{1,0:T(8,128)(2,1)S(1)} %slice.145), channel_id=1, source_target_pairs={{0,8},{2,10},{4,12},{6,14},{8,0},{10,2},{12,4},{14,6},{16,24},{18,... | collective-permute-start | bytes 1572872 | tf_op jit(solution)/shard_map/cond/branch_1_fun/ppermute | solution.py:20
  331.8 27.9 %collective-permute-start.8 = (bf16[256,1024]{1,0:T(8,128)(2,1)S(1)}, bf16[256,1024]{1,0:T(8,128)(2,1)S(1)}, u32[]{:S(2)}, u32[]{:S(2)}) collective-permute-start(bf16[256,1024]{1,0:T(8,128)(2,1)S(1)} %slice.119), channel_id=1, source_target_pairs={{0,8},{2,10},{4,12},{6,14},{8,0},{10,2},{12,4},{14,6},{16,24},{18,... | collective-permute-start | bytes 1572872 | tf_op jit(solution)/shard_map/cond/branch_1_fun/ppermute | solution.py:20
  348.6 14.7 %collective-permute-start.11 = (bf16[128,1024]{1,0:T(8,128)(2,1)S(1)}, bf16[128,1024]{1,0:T(8,128)(2,1)S(1)}, u32[]{:S(2)}, u32[]{:S(2)}) collective-permute-start(bf16[128,1024]{1,0:T(8,128)(2,1)S(1)} %slice.147), channel_id=1, source_target_pairs={{0,16},{2,18},{4,20},{6,22},{8,24},{10,26},{12,28},{14,30},{16,0},... | collective-permute-start | bytes 786440 | tf_op jit(solution)/shard_map/cond/branch_1_fun/ppermute | solution.py:20
  361.0 10.7 %collective-permute-start.9 = (bf16[128,1024]{1,0:T(8,128)(2,1)S(1)}, bf16[128,1024]{1,0:T(8,128)(2,1)S(1)}, u32[]{:S(2)}, u32[]{:S(2)}) collective-permute-start(bf16[128,1024]{1,0:T(8,128)(2,1)S(1)} %slice.143), channel_id=1, source_target_pairs={{0,16},{2,18},{4,20},{6,22},{8,24},{10,26},{12,28},{14,30},{16,0},... | collective-permute-start | bytes 786440 | tf_op jit(solution)/shard_map/cond/branch_1_fun/ppermute | solution.py:20
where the time goes:
time: 394 us; the launch traced here: 391 us
  waiting for transfers between devices  190 us (48%)
  Pallas kernels  62.5 us (16%)
  starting transfers between devices  53.6 us (14%)
  local copies, waits for them, and re-layouts  31.7 us (8%)
  matrix products  29.4 us (7%)
  other arithmetic  18.3 us (5%)
    ppermute x24, waiting for transfers between devices, permute(): return lax.ppermute(value, 'ep', pairs)  140 us
    ppermute x24, starting transfers between devices, permute(): return lax.ppermute(value, 'ep', pairs)  31.4 us
    dot_general x7, matrix products, dot(): lax.dot_general(a, b, ((dims[:1], dims[1:]), ((), ())), preferred_element...  29.4 us
    all_to_all x3, waiting for transfers between devices, spread(): lax.all_to_all(quarters, 'ep', 0, 0, tiled=True, axis_index_groups=planes())  23.9 us
    pallas_call x3, Pallas kernels, to_cross(): pl.pallas_call(kernel, out_shape=tuple((jax.ShapeDtypeStruct((slots,) + p...  14.1 us
    pallas_call x3, Pallas kernels, pick(): pl.pallas_call(kernel, out_shape=jax.ShapeDtypeStruct((4, width) + rest,...  14.1 us
    all_to_all x3, starting transfers between devices, spread(): lax.all_to_all(quarters, 'ep', 0, 0, tiled=True, axis_index_groups=planes())  13.5 us
    all_to_all x1, waiting for transfers between devices, collect(): lax.all_to_all(quarters, 'ep', 0, 0, tiled=True, axis_index_groups=planes())  10.3 us
  transfers between devices with their start and end apart: 30, of which 17 were waited for; matrix products, arithmetic and copies ran while one was open for 19% of the time, Pallas kernels for 12%

commit v1 on v0

--- a/solution.py
+++ b/solution.py
@@ -148,7 +148,23 @@
 
 
 def fourth_across(full, going):
-    return lax.cond(full, across, lambda going: going, going)
+    experts = lax.axis_size("ep")
+
+    def only(parity):
+        return [
+            (i, i ^ (experts // 2) if (i >> 2) % 2 == parity else i ^ 1) for i in range(experts)
+        ]
+
+    return lax.switch(
+        full,
+        (
+            lambda going: going,
+            lambda going: permute(going, only(0)),
+            lambda going: permute(going, only(1)),
+            across,
+        ),
+        going,
+    )
 
 
 def pick(facts, pool, came, fourth, *picked):
@@ -409,7 +425,8 @@
         for rnd, bit in enumerate((experts // 2, 1)):
             place = jnp.where(swap_flags[rnd] == 1, place[index ^ bit], place)
         facts = jnp.concatenate((facts, place[mine][None]))
-        full = jnp.any(jnp.sum(swap_flags[0].reshape(-1, 4), axis=1) > 3)
+        full = jnp.any(jnp.sum(swap_flags[0].reshape(-1, 2, 4), axis=2) > 3, axis=0)
+        full = jnp.sum(jnp.where(full, jnp.array([1, 2], jnp.int32), 0))
         return block, other, one, two, pool, to_cross(facts, pool), facts, full
 
     block, other, one, two, w_pool, w_going, facts, full = group(over_z, block, params[0])

time: 394 us -> 393 us (level)
  no operation moved by 1% of the time
where the time goes in v1:
time: 393 us; the launch traced here: 390 us
  waiting for transfers between devices  191 us (49%)
  Pallas kernels  59.5 us (15%)
  starting transfers between devices  54.6 us (14%)
  local copies, waits for them, and re-layouts  32.4 us (8%)
  matrix products  29.4 us (7%)
  other arithmetic  18.3 us (5%)
    ppermute x24, waiting for transfers between devices, permute(): return lax.ppermute(value, 'ep', pairs)  141 us
    ppermute x24, starting transfers between devices, permute(): return lax.ppermute(value, 'ep', pairs)  32.2 us
    dot_general x7, matrix products, dot(): lax.dot_general(a, b, ((dims[:1], dims[1:]), ((), ())), preferred_element...  29.4 us
    all_to_all x3, waiting for transfers between devices, spread(): lax.all_to_all(quarters, 'ep', 0, 0, tiled=True, axis_index_groups=planes())  23.8 us
    pallas_call x3, Pallas kernels, pick(): pl.pallas_call(kernel, out_shape=jax.ShapeDtypeStruct((4, width) + rest,...  14 us
    all_to_all x3, starting transfers between devices, spread(): lax.all_to_all(quarters, 'ep', 0, 0, tiled=True, axis_index_groups=planes())  13.5 us
    pallas_call x3, Pallas kernels, to_cross(): pl.pallas_call(kernel, out_shape=tuple((jax.ShapeDtypeStruct((slots,) + p...  11.3 us
    all_to_all x1, waiting for transfers between devices, collect(): lax.all_to_all(quarters, 'ep', 0, 0, tiled=True, axis_index_groups=planes())  10.8 us
  transfers between devices with their start and end apart: 30, of which 17 were waited for; matrix products, arithmetic and copies ran while one was open for 19% of the time, Pallas kernels for 12%

profile of v1, /device:TPU:0, one launch (start us, length us, event | category | flops | bytes accessed | tf_op | source)
XLA Modules:
  0.0 390.5 jit_solution(8130534196872658994)
XLA Ops:
  2.7 65.5 %conditional.11 = (bf16[2,272,1024]{2,1,0:T(8,128)(2,1)}, bf16[2,272,1024]{2,1,0:T(8,128)(2,1)S(1)}, bf16[2,272,1024]{2,1,0:T(8,128)(2,1)}, bf16[2,272,1024]{2,1...) conditional(s32[]{:T(128)} %bitcast.24, () %tuple.117, ...), branch_computations={%region_1.2_spmd, %region_2.10_spmd} | conditional | flops 1116584 | bytes 36579848 | solution.py:397
  2.7 4.1 %collective-permute-start.18 = (bf16[1,272,1024]{2,1,0:T(8,128)(2,1)S(1)}, bf16[1,272,1024]{2,1,0:T(8,128)(2,1)S(1)}, u32[]{:S(2)}, u32[]{:S(2)}) collective-permute-start(bf16[1,272,1024]{2,1,0:T(8,128)(2,1)S(1)} %bitcast.68), channel_id=1, source_target_pairs={{0,16},{2,18},{4,20},{6,22},{8,24},{10,26},{12,28},{14,30},{16,0},... | collective-permute-start | bytes 1671176 | tf_op jit(solution)/shard_map/cond/branch_1_fun/ppermute | solution.py:20
  6.8 1.6 collective-permute-start.19
  8.4 3.3 copy.41
  11.7 4.5 %all-to-all-start.4 = ((bf16[4,3,256,384]{3,2,1,0:T(8,128)(2,1)}), bf16[4,3,256,384]{3,2,1,0:T(8,128)(2,1)}, u32[]{:S(2)}, u32[]{:S(2)}) async-start(bf16[4,3,256,384]{3,2,1,0:T(8,128)(2,1)} %bitcast.63), calls=%async_computation.4 | async-start | bytes 4718592 | tf_op jit(solution)/shard_map/cond/branch_1_fun/all_to_all | solution.py:110
  17.7 13.7 %collective-permute-done.18 = bf16[1,272,1024]{2,1,0:T(8,128)(2,1)S(1)} collective-permute-done((bf16[1,272,1024]{2,1,0:T(8,128)(2,1)S(1)}, bf16[1,272,1024]{2,1,0:T(8,128)(2,1)S(1)}, u32[]{:S(2)}, u32[]{:S(2)}) %collective-permute-start.18) | collective-permute-done | bytes 557088 | tf_op jit(solution)/shard_map/cond/branch_1_fun/ppermute | solution.py:20
  32.6 1.5 collective-permute-start.21
  34.1 1.5 collective-permute-start.22
  39.4 10.2 %collective-permute-done.20 = bf16[1,272,1024]{2,1,0:T(8,128)(2,1)S(1)} collective-permute-done((bf16[1,272,1024]{2,1,0:T(8,128)(2,1)S(1)}, bf16[1,272,1024]{2,1,0:T(8,128)(2,1)S(1)}, u32[]{:S(2)}, u32[]{:S(2)}) %collective-permute-start.20) | collective-permute-done | bytes 557088 | tf_op jit(solution)/shard_map/cond/branch_1_fun/ppermute | solution.py:20
  49.7 3.7 branch_1_fun.9
  53.4 14.2 %collective-permute-done.21 = bf16[2,272,1024]{2,1,0:T(8,128)(2,1)} collective-permute-done((bf16[2,272,1024]{2,1,0:T(8,128)(2,1)}, bf16[2,272,1024]{2,1,0:T(8,128)(2,1)}, u32[]{:S(2)}, u32[]{:S(2)}) %collective-permute-start.21) | collective-permute-done | bytes 1114144 | tf_op jit(solution)/shard_map/cond/branch_1_fun/ppermute | solution.py:20
  69.3 84.9 %conditional.13 = (bf16[2,272,1024]{2,1,0:T(8,128)(2,1)}, bf16[2,272,1024]{2,1,0:T(8,128)(2,1)}, bf16[2,272,1024]{2,1,0:T(8,128)(2,1)}, bf16[2,272,1024]{2,1,0:T...) conditional(s32[]{:T(128)} %bitcast.24, () %tuple.120, ...), branch_computations={%region_10.11_spmd, %region_11.12_spmd} | conditional | bytes 34341112 | solution.py:397
  70.7 3.3 copy.40
  74.0 4.5 %all-to-all-start.1 = ((bf16[4,3,256,384]{3,2,1,0:T(8,128)(2,1)}), bf16[4,3,256,384]{3,2,1,0:T(8,128)(2,1)}, u32[]{:S(2)}, u32[]{:S(2)}) async-start(bf16[4,3,256,384]{3,2,1,0:T(8,128)(2,1)} %bitcast.62), calls=%async_computation.1 | async-start | bytes 4718592 | tf_op jit(solution)/shard_map/cond/branch_1_fun/all_to_all | solution.py:110
  78.5 2.0 collective-permute-start.12
  82.0 14.9 %collective-permute-done.11 = bf16[2,272,1024]{2,1,0:T(8,128)(2,1)} collective-permute-done((bf16[2,272,1024]{2,1,0:T(8,128)(2,1)S(1)}, bf16[2,272,1024]{2,1,0:T(8,128)(2,1)}, u32[]{:S(2)}, u32[]{:S(2)}) %collective-permute-start.11) | collective-permute-done | bytes 1114144 | tf_op jit(solution)/shard_map/cond/branch_1_fun/ppermute | solution.py:20
  98.4 23.8 %all-to-all-done.1.pool = bf16[4,3,256,384]{3,2,1,0:T(8,128)(2,1)} async-done(((bf16[4,3,256,384]{3,2,1,0:T(8,128)(2,1)}), bf16[4,3,256,384]{3,2,1,0:T(8,128)(2,1)}, u32[]{:S(2)}, u32[]{:S(2)}) %all-to-all-start.1) | async-done | bytes 2359328 | tf_op jit(solution)/shard_map/cond/branch_1_fun/all_to_all | solution.py:110
  122.2 3.9 branch_1_fun.10
  126.1 5.4 %collective-permute-done.12 = bf16[2,272,1024]{2,1,0:T(8,128)(2,1)} collective-permute-done((bf16[2,272,1024]{2,1,0:T(8,128)(2,1)S(1)}, bf16[2,272,1024]{2,1,0:T(8,128)(2,1)}, u32[]{:S(2)}, u32[]{:S(2)}) %collective-permute-start.12) | collective-permute-done | bytes 1114144 | tf_op jit(solution)/shard_map/cond/branch_1_fun/ppermute | solution.py:20
  131.5 13.2 %collective-permute-done.10 = bf16[2,272,1024]{2,1,0:T(8,128)(2,1)} collective-permute-done((bf16[2,272,1024]{2,1,0:T(8,128)(2,1)}, bf16[2,272,1024]{2,1,0:T(8,128)(2,1)}, u32[]{:S(2)}, u32[]{:S(2)}) %collective-permute-start.10) | collective-permute-done | bytes 1114144 | tf_op jit(solution)/shard_map/cond/branch_1_fun/ppermute | solution.py:20
  144.8 9.4 %collective-permute-done.13 = bf16[2,272,1024]{2,1,0:T(8,128)(2,1)} collective-permute-done((bf16[2,272,1024]{2,1,0:T(8,128)(2,1)}, bf16[2,272,1024]{2,1,0:T(8,128)(2,1)}, u32[]{:S(2)}, u32[]{:S(2)}) %collective-permute-start.13) | collective-permute-done | bytes 1114144 | tf_op jit(solution)/shard_map/cond/branch_1_fun/ppermute | solution.py:20
  154.1 1.7 collective-permute-start.32
  157.2 38.8 %conditional.14 = (bf16[3,1024,384]{2,1,0:T(8,128)(2,1)S(1)}, bf16[2048,1024]{1,0:T(8,128)(2,1)}, bf16[2048,1024]{1,0:T(8,128)(2,1)}, f32[2048,1]{0,1:T(1,128)S(1)}, bf16[4,3,256,384]{3,2,0,1:T(8,128)(2,1)}) conditional(s32[]{:T(128)} %bitcast.24, () %tuple.116, (s32[17]{0:T(128)}, bf16[4,3,256,384]{3,2,1,0:T(8,128)(2,1)}, ...), branch_computations={%region_16.17_spmd, %region_17.19_spmd} | conditional | flops 6301699 | bytes 76640512 | solution.py:397
  157.2 4.8 %branch_1_fun.11 = bf16[4,3,256,384]{3,2,1,0:T(8,128)(2,1)} custom-call(s32[17]{0:T(128)} %get-tuple-element.148.facts, bf16[4,3,256,384]{3,2,1,0:T(8,128)(2,1)} %get-tuple-element.149.pool, bf16[3,3,256,384]{3,2,1,0:T(8,128)(2,1)} %get-tuple-element.150.came, bf16[1,3,256,384]{3,2,1,0:T(8,128)(2,1)S(1)} %get-tuple-element.151.fourth), custom_call_target="tpu_custom_call" | custom-call | bytes 7077888 | tf_op jit(solution)/shard_map/cond/branch_1_fun/pallas_call | solution.py:198
  162.0 3.8 all-to-all-start.2
  168.4 5.5 %branch_1_fun.12 = (bf16[16,128,1024]{2,1,0:T(8,128)(2,1)}, bf16[16,128,1024]{2,1,0:T(8,128)(2,1)S(1)}, bf16[16,16,1024]{2,1,0:T(8,128)(2,1)S(1)}) custom-call(bf16[2,272,1024]{2,1,0:T(8,128)(2,1)} %get-tuple-element.152.refs_0_, bf16[2,272,1024]{2,1,0:T(8,128)(2,1)S(1)} %copy-done.6, bf16[2,272,1024]{2,1,0:T(8,128)(2,1)} %get-tuple-element.154.refs_2_, ...), custom_call_target="tpu_custom_call" | custom-call | bytes 17825792 | tf_op jit(solution)/shard_map/cond/branch_1_fun/pallas_call | solution.py:237
  173.9 2.0 copy-done.1
  176.9 5.0 %fusion = bf16[2048,1024]{1,0:T(8,128)(2,1)} fusion(bf16[16,128,1024]{2,1,0:T(8,128)(2,1)} %copy-done.1, f32[2048]{0:T(1024)S(1)} %bitcast.71), kind=kLoop, calls=%fused_computation.4 | loop fusion | flops 6291456 | bytes 8396800 | tf_op jit(solution)/shard_map/cond/branch_1_fun/convert_element_type | solution.py:459
  181.9 10.8 %all-to-all-done.2 = bf16[4,3,256,384]{3,2,1,0:T(8,128)(2,1)S(1)} async-done(((bf16[4,3,256,384]{3,2,1,0:T(8,128)(2,1)}), bf16[4,3,256,384]{3,2,1,0:T(8,128)(2,1)S(1)}, u32[]{:S(2)}, u32[]{:S(2)}) %all-to-all-start.2) | async-done | bytes 2359328 | tf_op jit(solution)/shard_map/cond/branch_1_fun/all_to_all | solution.py:336
  194.1 1.9 copy.32
  196.1 36.5 %conditional.15 = (bf16[2048,384]{1,0:T(8,128)(2,1)}, bf16[2048,384]{1,0:T(8,128)(2,1)}, bf16[2048,384]{1,0:T(8,128)(2,1)}, bf16[2048,512]{1,0:T(8,128)(2,1)}, b...) conditional(s32[]{:T(128)} %bitcast.24, () %tuple.115, (s32[2,16]{1,0:T(2,128)S(1)}, ...), branch_computations={%region_19.20_spmd, %region_20.23_spmd} | conditional | flops 6442450944 | bytes 74727584 | solution.py:397
  196.1 3.3 copy.36
  199.4 4.5 %all-to-all-start = ((bf16[4,3,256,384]{3,2,1,0:T(8,128)(2,1)}), bf16[4,3,256,384]{3,2,1,0:T(8,128)(2,1)}, u32[]{:S(2)}, u32[]{:S(2)}) async-start(bf16[4,3,256,384]{3,2,1,0:T(8,128)(2,1)} %copy.36), calls=%async_computation | async-start | bytes 4718592 | tf_op jit(solution)/shard_map/cond/branch_1_fun/all_to_all | solution.py:110
  205.5 10.1 %branch_1_fun.13 = bf16[3,2048,384]{2,1,0:T(8,128)(2,1)S(1)} custom-call(bf16[2048,1024]{1,0:T(8,128)(2,1)} %get-tuple-element.165.x_rows, bf16[2048,1024]{1,0:T(8,128)(2,1)} %get-tuple-element.166.dy_rows, bf16[3,1024,384]{2,1,0:T(8,128)(2,1)S(1)} %get-tuple-element.167.weight.refs_3_), custom_call_target="tpu_custom_call" | custom-call | flops 4831838208 | bytes 15466496 | tf_op jit(solution)/shard_map/cond/branch_1_fun/pallas_call | solution.py:263
  215.6 8.1 %conditional = (bf16[3,2048,384]{2,1,0:T(8,128)(2,1)S(1)}, bf16[3,2048,384]{2,1,0:T(8,128)(2,1)}) conditional(s32[]{:T(128)} %bitcast.19, () %tuple.84, bf16[3,2048,384]{2,1,0:T(8,128)(2,1)S(1)} %branch_1_fun.13), branch_computations={%region_21.21_spmd, %region_22.22_spmd} | conditional | bytes 28311608 | solution.py:397
  216.2 7.5 %collective-permute-done.3 = bf16[3,2048,384]{2,1,0:T(8,128)(2,1)} collective-permute-done((bf16[3,2048,384]{2,1,0:T(8,128)(2,1)S(1)}, bf16[3,2048,384]{2,1,0:T(8,128)(2,1)}, u32[]{:S(2)}, u32[]{:S(2)}) %collective-permute-start.3) | collective-permute-done | bytes 4718624 | tf_op jit(solution)/shard_map/cond/branch_1_fun/cond/branch_1_fun/ppermute | solution.py:30
  223.7 8.8 %branch_1_fun.14 = (bf16[2048,384]{1,0:T(8,128)(2,1)}, bf16[2048,384]{1,0:T(8,128)(2,1)}, bf16[2048,384]{1,0:T(8,128)(2,1)}, bf16[2048,512]{1,0:T(8,128)(2,1)}, bf16[2048,512]{1,0:T(8,128)(2,1)}) custom-call(bf16[3,2048,384]{2,1,0:T(8,128)(2,1)S(1)} %get-tuple-element.168.refs_0_, bf16[3,2048,384]{2,1,0:T(8,128)(2,1)} %get-tuple-element.169.refs_1_, ...), custom_call_target="tpu_custom_call" | custom-call | flops 1610612736 | bytes 19136512 | tf_op jit(solution)/shard_map/cond/branch_1_fun/pallas_call | solution.py:315
  232.6 3.7 conditional.17
  232.7 3.7 branch_1_fun.15
  237.7 80.7 %conditional.18 = (bf16[512,1024]{1,0:T(8,128)(2,1)}, bf16[512,1024]{0,1:T(8,128)(2,1)}, f32[1024,384]{1,0:T(8,128)}, f32[1024,384]{1,0:T(8,128)}, f32[1024,384]...) conditional(s32[]{:T(128)} %bitcast.24, () %tuple.114, (bf16[2048,512]{1,0:T(8,128)(2,1)}, ...), branch_computations={%region_33.34_spmd, %region_34.35_spmd} | conditional | flops 8071938048 | bytes 110362992 | solution.py:397
  239.0 2.0 collective-permute-start.23
  242.3 1.5 collective-permute-start.24
  243.9 2.7 fusion.5
  246.6 2.7 fusion.2
  249.2 2.7 add_convert_fusion.1
  252.1 2.7 add_convert_fusion
  254.9 6.2 %fusion.16 = f32[1024,384]{1,0:T(8,128)} fusion(bf16[2048,1024]{1,0:T(8,128)(2,1)} %get-tuple-element.188, bf16[2048,384]{1,0:T(8,128)(2,1)} %get-tuple-element.180), kind=kOutput, calls=%fused_computation.68 | convolution fusion | flops 1610612736 | bytes 7340032 | tf_op jit(solution)/shard_map/cond/branch_1_fun/dot_general | solution.py:366
  261.1 6.3 %fusion.17 = f32[1024,384]{1,0:T(8,128)} fusion(bf16[2048,1024]{1,0:T(8,128)(2,1)} %get-tuple-element.188, bf16[2048,384]{1,0:T(8,128)(2,1)} %get-tuple-element.182), kind=kOutput, calls=%fused_computation.69 | convolution fusion | flops 1610612736 | bytes 7340032 | tf_op jit(solution)/shard_map/cond/branch_1_fun/dot_general | solution.py:366
  271.2 6.2 %fusion.18 = f32[1024,384]{1,0:T(8,128)} fusion(bf16[2048,1024]{1,0:T(8,128)(2,1)} %get-tuple-element.189, bf16[2048,384]{1,0:T(8,128)(2,1)} %get-tuple-element.190), kind=kOutput, calls=%fused_computation.70 | convolution fusion | flops 1610612736 | bytes 7340032 | tf_op jit(solution)/shard_map/cond/branch_1_fun/dot_general | solution.py:366
  277.3 5.0 %branch_1_fun.16 = bf16[4,3,256,384]{3,2,1,0:T(8,128)(2,1)} custom-call(s32[17]{0:T(128)} %get-tuple-element.191.facts, bf16[4,3,256,384]{3,2,1,0:T(8,128)(2,1)} %get-tuple-element.192.pool, bf16[3,3,256,384]{3,2,1,0:T(8,128)(2,1)} %get-tuple-element.193.came, bf16[1,3,256,384]{3,2,1,0:T(8,128)(2,1)} %get-tuple-element.194.fourth), custom_call_target="tpu_custom_call" | custom-call | bytes 7077888 | tf_op jit(solution)/shard_map/cond/branch_1_fun/pallas_call | solution.py:198
  283.5 1.5 collective-permute-start.26
  285.0 18.2 %collective-permute-done.25 = bf16[512,512]{1,0:T(8,128)(2,1)S(1)} collective-permute-done((bf16[512,512]{1,0:T(8,128)(2,1)S(1)}, bf16[512,512]{1,0:T(8,128)(2,1)S(1)}, u32[]{:S(2)}, u32[]{:S(2)}) %collective-permute-start.25) | collective-permute-done | bytes 524320 | tf_op jit(solution)/shard_map/cond/branch_1_fun/ppermute | solution.py:20
  305.4 1.6 collective-permute-start.30
  309.4 7.4 %collective-permute-done.28 = bf16[512,512]{0,1:T(8,128)(2,1)S(1)} collective-permute-done((bf16[512,512]{0,1:T(8,128)(2,1)S(1)}, bf16[512,512]{0,1:T(8,128)(2,1)S(1)}, u32[]{:S(2)}, u32[]{:S(2)}) %collective-permute-start.28) | collective-permute-done | bytes 524320 | tf_op jit(solution)/shard_map/cond/branch_1_fun/ppermute | solution.py:20
  318.4 62.3 %conditional.20 = (bf16[128,1024]{1,0:T(8,128)(2,1)}, bf16[128,1024]{1,0:T(8,128)(2,1)}, bf16[4,6,256,384]{3,2,1,0:T(8,128)(2,1)}) conditional(s32[]{:T(128)} %bitcast.24, () %tuple.113, (bf16[512,1024]{1,0:T(8,128)(2,1)}, bf16[512,1024]{0,1:T(8,128)(2,1)}, s32[17]{0:T(128)}, bf16[4,3,256,384]{3,2,1,0:T(8,128)(2,1)}, ...), branch_computations={%region_35.36_spmd, %region_36.37_spmd} | conditional | flops 3145728 | bytes 61079796 | solution.py:397
  318.4 4.3 %branch_1_fun.17 = bf16[4,6,256,384]{3,2,1,0:T(8,128)(2,1)S(1)} custom-call(s32[17]{0:T(128)} %get-tuple-element.197.facts, bf16[4,3,256,384]{3,2,1,0:T(8,128)(2,1)} %get-tuple-element.198.pool, bf16[3,3,256,384]{3,2,1,0:T(8,128)(2,1)} %get-tuple-element.199.came, bf16[1,3,256,384]{3,2,1,0:T(8,128)(2,1)S(1)} %get-tuple-element.200.fourth, ...), custom_call_target="tpu_custom_call" | custom-call | bytes 11796480 | tf_op jit(solution)/shard_map/cond/branch_1_fun/pallas_call | solution.py:198
  322.7 2.2 copy-done
  324.8 4.9 %all-to-all-start.3 = ((bf16[4,6,256,384]{3,2,1,0:T(8,128)(2,1)}), bf16[4,6,256,384]{3,2,1,0:T(8,128)(2,1)}, u32[]{:S(2)}, u32[]{:S(2)}) async-start(bf16[4,6,256,384]{3,2,1,0:T(8,128)(2,1)} %copy-done), calls=%async_computation.3 | async-start | bytes 9437184 | tf_op jit(solution)/shard_map/cond/branch_1_fun/all_to_all | solution.py:506
  334.5 14.5 %collective-permute-done.16 = bf16[256,1024]{1,0:T(8,128)(2,1)S(1)} collective-permute-done((bf16[256,1024]{1,0:T(8,128)(2,1)S(1)}, bf16[256,1024]{1,0:T(8,128)(2,1)S(1)}, u32[]{:S(2)}, u32[]{:S(2)}) %collective-permute-start.16) | collective-permute-done | bytes 524320 | tf_op jit(solution)/shard_map/cond/branch_1_fun/ppermute | solution.py:20
  349.8 9.2 %collective-permute-done.14 = bf16[256,1024]{1,0:T(8,128)(2,1)S(1)} collective-permute-done((bf16[256,1024]{1,0:T(8,128)(2,1)S(1)}, bf16[256,1024]{1,0:T(8,128)(2,1)S(1)}, u32[]{:S(2)}, u32[]{:S(2)}) %collective-permute-start.14) | collective-permute-done | bytes 524320 | tf_op jit(solution)/shard_map/cond/branch_1_fun/ppermute | solution.py:20
  360.7 3.3 collective-permute-done.17
  364.7 7.2 %collective-permute-done.15 = bf16[128,1024]{1,0:T(8,128)(2,1)S(1)} collective-permute-done((bf16[128,1024]{1,0:T(8,128)(2,1)S(1)}, bf16[128,1024]{1,0:T(8,128)(2,1)S(1)}, u32[]{:S(2)}, u32[]{:S(2)}) %collective-permute-start.15) | collective-permute-done | bytes 262176 | tf_op jit(solution)/shard_map/cond/branch_1_fun/ppermute | solution.py:20
  372.7 7.9 %all-to-all-done.3 = bf16[4,6,256,384]{3,2,1,0:T(8,128)(2,1)} async-done(((bf16[4,6,256,384]{3,2,1,0:T(8,128)(2,1)}), bf16[4,6,256,384]{3,2,1,0:T(8,128)(2,1)}, u32[]{:S(2)}, u32[]{:S(2)}) %all-to-all-start.3) | async-done | bytes 4718624 | tf_op jit(solution)/shard_map/cond/branch_1_fun/all_to_all | solution.py:506
  380.6 9.9 %shard_map.142 = (bf16[1,3,1024,384]{3,2,1,0:T(8,128)(2,1)}, bf16[1,3,1024,384]{3,2,1,0:T(8,128)(2,1)}, bf16[1,3,1024,384]{3,2,1,0:T(8,128)(2,1)}) custom-call(bf16[3,1024,384]{2,1,0:T(8,128)(2,1)S(1)} %get-tuple-element.277.weight, bf16[4,6,256,384]{3,2,1,0:T(8,128)(2,1)} %get-tuple-element.302.moments, f32[1024,384]{1,0:T(8,128)} %get-tuple-element.303.grad_gate, ...), custom_call_target="tpu_custom_call" | custom-call | flops 47185920 | bytes 18874368 | tf_op jit(solution)/shard_map/pallas_call | solution.py:53
  (119 shorter events, 42.8 us)
Async XLA Ops:
  0.6 0.7 copy-start.13
  0.6 0.7 copy-start.12
  0.7 0.8 copy-start.11
  0.7 2.0 copy-start.8
  0.7 2.0 copy-start.7
  0.7 2.0 copy-start.2
  2.7 28.8 %collective-permute-start.18 = (bf16[1,272,1024]{2,1,0:T(8,128)(2,1)S(1)}, bf16[1,272,1024]{2,1,0:T(8,128)(2,1)S(1)}, u32[]{:S(2)}, u32[]{:S(2)}) collective-permute-start(bf16[1,272,1024]{2,1,0:T(8,128)(2,1)S(1)} %bitcast.68), channel_id=1, source_target_pairs={{0,16},{2,18},{4,20},{6,22},{8,24},{10,26},{12,28},{14,30},{16,0},... | collective-permute-start | bytes 1671176 | tf_op jit(solution)/shard_map/cond/branch_1_fun/ppermute | solution.py:20
  6.8 32.6 %collective-permute-start.19 = (bf16[1,272,1024]{2,1,0:T(8,128)(2,1)S(1)}, bf16[1,272,1024]{2,1,0:T(8,128)(2,1)S(1)}, u32[]{:S(2)}, u32[]{:S(2)}) collective-permute-start(bf16[1,272,1024]{2,1,0:T(8,128)(2,1)S(1)} %bitcast.69), channel_id=1, source_target_pairs={{0,8},{2,10},{4,12},{6,14},{8,0},{10,2},{12,4},{14,6},{16,24},{18,... | collective-permute-start | bytes 1671176 | tf_op jit(solution)/shard_map/cond/branch_1_fun/ppermute | solution.py:20
  11.7 38.0 %all-to-all-start.4 = ((bf16[4,3,256,384]{3,2,1,0:T(8,128)(2,1)}), bf16[4,3,256,384]{3,2,1,0:T(8,128)(2,1)}, u32[]{:S(2)}, u32[]{:S(2)}) async-start(bf16[4,3,256,384]{3,2,1,0:T(8,128)(2,1)} %bitcast.63), calls=%async_computation.4 | async-start | bytes 4718592 | tf_op jit(solution)/shard_map/cond/branch_1_fun/all_to_all | solution.py:110
  16.3 22.5 %copy-start.14 = (s32[2]{0:T(128)S(1)}, s32[2]{0:T(128)}, u32[]{:S(2)}) copy-start(s32[2]{0:T(128)} %constant.74.clone.1) | copy-start | bytes 28 | tf_op jit(solution)/shard_map/cond
  32.6 35.0 %collective-permute-start.21 = (bf16[2,272,1024]{2,1,0:T(8,128)(2,1)}, bf16[2,272,1024]{2,1,0:T(8,128)(2,1)}, u32[]{:S(2)}, u32[]{:S(2)}) collective-permute-start(bf16[2,272,1024]{2,1,0:T(8,128)(2,1)} %pad_maximum_fusion.2), channel_id=1, source_target_pairs={{0,2},{2,0},{4,6},{6,4},{8,10},{10,8},{12,14},{14,12},{16,18},{18,... | collective-permute-start | bytes 3342344 | tf_op jit(solution)/shard_map/cond/branch_1_fun/ppermute | solution.py:20
  34.1 33.5 %collective-permute-start.22 = (bf16[2,272,1024]{2,1,0:T(8,128)(2,1)}, bf16[2,272,1024]{2,1,0:T(8,128)(2,1)}, u32[]{:S(2)}, u32[]{:S(2)}) collective-permute-start(bf16[2,272,1024]{2,1,0:T(8,128)(2,1)} %pad_maximum_fusion.2), channel_id=1, source_target_pairs={{0,4},{2,6},{4,0},{6,2},{8,12},{10,14},{12,8},{14,10},{16,20},{18,... | collective-permute-start | bytes 3342344 | tf_op jit(solution)/shard_map/cond/branch_1_fun/ppermute | solution.py:20
  36.6 13.0 %collective-permute-start.20 = (bf16[1,272,1024]{2,1,0:T(8,128)(2,1)S(1)}, bf16[1,272,1024]{2,1,0:T(8,128)(2,1)S(1)}, u32[]{:S(2)}, u32[]{:S(2)}) collective-permute-start(bf16[1,272,1024]{2,1,0:T(8,128)(2,1)S(1)} %collective-permute-done.18), channel_id=1, source_target_pairs={{0,8},{2,10},{4,12},{6,14},{8,0},{10,2},{12,4},{14,6},{16,24},{18,... | collective-permute-start | bytes 1671176 | tf_op jit(solution)/shard_map/cond/branch_1_fun/ppermute | solution.py:20
  68.2 1.0 copy-start.5
  68.3 85.9 %collective-permute-start.31 = (bf16[3,3,256,384]{3,2,1,0:T(8,128)(2,1)}, bf16[3,3,256,384]{3,2,1,0:T(8,128)(2,1)}, u32[]{:S(2)}, u32[]{:S(2)}) collective-permute-start(bf16[3,3,256,384]{3,2,1,0:T(8,128)(2,1)} %get-tuple-element.260), channel_id=1, source_target_pairs={{0,16},{2,18},{4,20},{6,22},{8,24},{10,26},{12,28},{14,30},{16,0},... | collective-permute-start | bytes 5308424 | tf_op jit(solution)/shard_map/ppermute | solution.py:20
  69.3 27.6 %collective-permute-start.11 = (bf16[2,272,1024]{2,1,0:T(8,128)(2,1)S(1)}, bf16[2,272,1024]{2,1,0:T(8,128)(2,1)}, u32[]{:S(2)}, u32[]{:S(2)}) collective-permute-start(bf16[2,272,1024]{2,1,0:T(8,128)(2,1)S(1)} %get-tuple-element.143), channel_id=1, source_target_pairs={{0,2},{2,0},{4,6},{6,4},{8,10},{10,8},{12,14},{14,12},{16,18},{18,... | collective-permute-start | bytes 3342344 | tf_op jit(solution)/shard_map/cond/branch_1_fun/ppermute | solution.py:20
  74.0 48.2 %all-to-all-start.1 = ((bf16[4,3,256,384]{3,2,1,0:T(8,128)(2,1)}), bf16[4,3,256,384]{3,2,1,0:T(8,128)(2,1)}, u32[]{:S(2)}, u32[]{:S(2)}) async-start(bf16[4,3,256,384]{3,2,1,0:T(8,128)(2,1)} %bitcast.62), calls=%async_computation.1 | async-start | bytes 4718592 | tf_op jit(solution)/shard_map/cond/branch_1_fun/all_to_all | solution.py:110
  78.5 53.0 %collective-permute-start.12 = (bf16[2,272,1024]{2,1,0:T(8,128)(2,1)S(1)}, bf16[2,272,1024]{2,1,0:T(8,128)(2,1)}, u32[]{:S(2)}, u32[]{:S(2)}) collective-permute-start(bf16[2,272,1024]{2,1,0:T(8,128)(2,1)S(1)} %get-tuple-element.143), channel_id=1, source_target_pairs={{0,4},{2,6},{4,0},{6,2},{8,12},{10,14},{12,8},{14,10},{16,20},{18,... | collective-permute-start | bytes 3342344 | tf_op jit(solution)/shard_map/cond/branch_1_fun/ppermute | solution.py:20
  80.5 64.3 %collective-permute-start.10 = (bf16[2,272,1024]{2,1,0:T(8,128)(2,1)}, bf16[2,272,1024]{2,1,0:T(8,128)(2,1)}, u32[]{:S(2)}, u32[]{:S(2)}) collective-permute-start(bf16[2,272,1024]{2,1,0:T(8,128)(2,1)} %get-tuple-element.142), channel_id=1, source_target_pairs={{0,2},{2,0},{4,6},{6,4},{8,10},{10,8},{12,14},{14,12},{16,18},{18,... | collective-permute-start | bytes 3342344 | tf_op jit(solution)/shard_map/cond/branch_1_fun/ppermute | solution.py:20
  96.9 57.3 %collective-permute-start.13 = (bf16[2,272,1024]{2,1,0:T(8,128)(2,1)}, bf16[2,272,1024]{2,1,0:T(8,128)(2,1)}, u32[]{:S(2)}, u32[]{:S(2)}) collective-permute-start(bf16[2,272,1024]{2,1,0:T(8,128)(2,1)} %collective-permute-done.11), channel_id=1, source_target_pairs={{0,4},{2,6},{4,0},{6,2},{8,12},{10,14},{12,8},{14,10},{16,20},{18,... | collective-permute-start | bytes 3342344 | tf_op jit(solution)/shard_map/cond/branch_1_fun/ppermute | solution.py:20
  154.1 1.7 copy-start.3
  154.1 82.2 %collective-permute-start.32 = (bf16[3,3,256,384]{3,2,1,0:T(8,128)(2,1)}, bf16[3,3,256,384]{3,2,1,0:T(8,128)(2,1)}, u32[]{:S(2)}, u32[]{:S(2)}) collective-permute-start(bf16[3,3,256,384]{3,2,1,0:T(8,128)(2,1)} %get-tuple-element.286), channel_id=1, source_target_pairs={{0,16},{2,18},{4,20},{6,22},{8,24},{10,26},{12,28},{14,30},{16,0},... | collective-permute-start | bytes 5308424 | tf_op jit(solution)/shard_map/ppermute | solution.py:20
  162.0 6.3 %copy-start.6 = (bf16[2,272,1024]{2,1,0:T(8,128)(2,1)S(1)}, bf16[2,272,1024]{2,1,0:T(8,128)(2,1)}, u32[]{:S(2)}) copy-start(bf16[2,272,1024]{2,1,0:T(8,128)(2,1)} %get-tuple-element.153.refs_1_) | copy-start | bytes 3342340 | tf_op jit(solution)/shard_map/cond
  162.0 30.7 %all-to-all-start.2 = ((bf16[4,3,256,384]{3,2,1,0:T(8,128)(2,1)}), bf16[4,3,256,384]{3,2,1,0:T(8,128)(2,1)S(1)}, u32[]{:S(2)}, u32[]{:S(2)}) async-start(bf16[4,3,256,384]{3,2,1,0:T(8,128)(2,1)} %branch_1_fun.11), calls=%async_computation.2 | async-start | bytes 4718592 | tf_op jit(solution)/shard_map/cond/branch_1_fun/all_to_all | solution.py:336
  173.9 2.0 copy-start.1
  176.9 5.0 %copy-start.9 = (f32[16,128]{1,0:T(8,128)}, f32[16,128]{1,0:T(8,128)S(1)}, u32[]{:S(2)}) copy-start(f32[16,128]{1,0:T(8,128)S(1)} %convert_reduce_fusion) | copy-start | bytes 24580 | tf_op jit(solution)/shard_map/cond
  192.7 1.4 copy-start.4
  194.1 2.0 copy-start.10
  199.4 33.1 %all-to-all-start = ((bf16[4,3,256,384]{3,2,1,0:T(8,128)(2,1)}), bf16[4,3,256,384]{3,2,1,0:T(8,128)(2,1)}, u32[]{:S(2)}, u32[]{:S(2)}) async-start(bf16[4,3,256,384]{3,2,1,0:T(8,128)(2,1)} %copy.36), calls=%async_computation | async-start | bytes 4718592 | tf_op jit(solution)/shard_map/cond/branch_1_fun/all_to_all | solution.py:110
  215.6 8.1 %collective-permute-start.3 = (bf16[3,2048,384]{2,1,0:T(8,128)(2,1)S(1)}, bf16[3,2048,384]{2,1,0:T(8,128)(2,1)}, u32[]{:S(2)}, u32[]{:S(2)}) collective-permute-start(bf16[3,2048,384]{2,1,0:T(8,128)(2,1)S(1)} %param.12), channel_id=1, source_target_pairs={{0,1},{1,0},{2,3},{3,2},{4,5},{5,4},{6,7},{7,6},{8,9},{9,8},{10,11... | collective-permute-start | bytes 14155784 | tf_op jit(solution)/shard_map/cond/branch_1_fun/cond/branch_1_fun/ppermute | solution.py:30
  236.3 82.0 %collective-permute-start.33 = (bf16[3,3,256,384]{3,2,1,0:T(8,128)(2,1)}, bf16[3,3,256,384]{3,2,1,0:T(8,128)(2,1)}, u32[]{:S(2)}, u32[]{:S(2)}) collective-permute-start(bf16[3,3,256,384]{3,2,1,0:T(8,128)(2,1)} %get-tuple-element.295), channel_id=1, source_target_pairs={{0,16},{2,18},{4,20},{6,22},{8,24},{10,26},{12,28},{14,30},{16,0},... | collective-permute-start | bytes 5308424 | tf_op jit(solution)/shard_map/ppermute | solution.py:20
  239.0 28.3 %collective-permute-start.23 = (bf16[1024,512]{1,0:T(8,128)(2,1)S(1)}, bf16[1024,512]{1,0:T(8,128)(2,1)S(1)}, u32[]{:S(2)}, u32[]{:S(2)}) collective-permute-start(bf16[1024,512]{1,0:T(8,128)(2,1)S(1)} %slice.101), channel_id=1, source_target_pairs={{0,2},{2,0},{4,6},{6,4},{8,10},{10,8},{12,14},{14,12},{16,18},{18,... | collective-permute-start | bytes 3145736 | tf_op jit(solution)/shard_map/cond/branch_1_fun/ppermute | solution.py:20
  242.3 25.0 %collective-permute-start.24 = (bf16[1024,512]{1,0:T(8,128)(2,1)S(1)}, bf16[1024,512]{1,0:T(8,128)(2,1)S(1)}, u32[]{:S(2)}, u32[]{:S(2)}) collective-permute-start(bf16[1024,512]{1,0:T(8,128)(2,1)S(1)} %slice.102), channel_id=1, source_target_pairs={{0,4},{2,6},{4,0},{6,2},{8,12},{10,14},{12,8},{14,10},{16,20},{18,... | collective-permute-start | bytes 3145736 | tf_op jit(solution)/shard_map/cond/branch_1_fun/ppermute | solution.py:20
  267.3 37.1 %collective-permute-start.27 = (bf16[1024,512]{0,1:T(8,128)(2,1)S(1)}, bf16[1024,512]{0,1:T(8,128)(2,1)S(1)}, u32[]{:S(2)}, u32[]{:S(2)}) collective-permute-start(bf16[1024,512]{0,1:T(8,128)(2,1)S(1)} %slice.132), channel_id=1, source_target_pairs={{0,2},{2,0},{4,6},{6,4},{8,10},{10,8},{12,14},{14,12},{16,18},{18,... | collective-permute-start | bytes 3145736 | tf_op jit(solution)/shard_map/cond/branch_1_fun/ppermute | solution.py:20
  267.9 37.4 %collective-permute-start.29 = (bf16[1024,512]{0,1:T(8,128)(2,1)S(1)}, bf16[1024,512]{0,1:T(8,128)(2,1)S(1)}, u32[]{:S(2)}, u32[]{:S(2)}) collective-permute-start(bf16[1024,512]{0,1:T(8,128)(2,1)S(1)} %slice.133), channel_id=1, source_target_pairs={{0,4},{2,6},{4,0},{6,2},{8,12},{10,14},{12,8},{14,10},{16,20},{18,... | collective-permute-start | bytes 3145736 | tf_op jit(solution)/shard_map/cond/branch_1_fun/ppermute | solution.py:20
  270.2 33.0 %collective-permute-start.25 = (bf16[512,512]{1,0:T(8,128)(2,1)S(1)}, bf16[512,512]{1,0:T(8,128)(2,1)S(1)}, u32[]{:S(2)}, u32[]{:S(2)}) collective-permute-start(bf16[512,512]{1,0:T(8,128)(2,1)S(1)} %add_convert_fusion.9), channel_id=1, source_target_pairs={{0,4},{2,6},{4,0},{6,2},{8,12},{10,14},{12,8},{14,10},{16,20},{18,... | collective-permute-start | bytes 1572872 | tf_op jit(solution)/shard_map/cond/branch_1_fun/ppermute | solution.py:20
  283.5 23.5 %collective-permute-start.26 = (bf16[512,512]{1,0:T(8,128)(2,1)S(1)}, bf16[512,512]{1,0:T(8,128)(2,1)S(1)}, u32[]{:S(2)}, u32[]{:S(2)}) collective-permute-start(bf16[512,512]{1,0:T(8,128)(2,1)S(1)} %add_convert_fusion.7), channel_id=1, source_target_pairs={{0,2},{2,0},{4,6},{6,4},{8,10},{10,8},{12,14},{14,12},{16,18},{18,... | collective-permute-start | bytes 1572872 | tf_op jit(solution)/shard_map/cond/branch_1_fun/ppermute | solution.py:20
  304.7 12.1 %collective-permute-start.28 = (bf16[512,512]{0,1:T(8,128)(2,1)S(1)}, bf16[512,512]{0,1:T(8,128)(2,1)S(1)}, u32[]{:S(2)}, u32[]{:S(2)}) collective-permute-start(bf16[512,512]{0,1:T(8,128)(2,1)S(1)} %add_convert_fusion.5), channel_id=1, source_target_pairs={{0,4},{2,6},{4,0},{6,2},{8,12},{10,14},{12,8},{14,10},{16,20},{18,... | collective-permute-start | bytes 1572872 | tf_op jit(solution)/shard_map/cond/branch_1_fun/ppermute | solution.py:20
  305.4 11.7 %collective-permute-start.30 = (bf16[512,512]{0,1:T(8,128)(2,1)S(1)}, bf16[512,512]{0,1:T(8,128)(2,1)S(1)}, u32[]{:S(2)}, u32[]{:S(2)}) collective-permute-start(bf16[512,512]{0,1:T(8,128)(2,1)S(1)} %add_convert_fusion.3), channel_id=1, source_target_pairs={{0,2},{2,0},{4,6},{6,4},{8,10},{10,8},{12,14},{14,12},{16,18},{18,... | collective-permute-start | bytes 1572872 | tf_op jit(solution)/shard_map/cond/branch_1_fun/ppermute | solution.py:20
  322.6 2.2 copy-start
  324.8 55.8 %all-to-all-start.3 = ((bf16[4,6,256,384]{3,2,1,0:T(8,128)(2,1)}), bf16[4,6,256,384]{3,2,1,0:T(8,128)(2,1)}, u32[]{:S(2)}, u32[]{:S(2)}) async-start(bf16[4,6,256,384]{3,2,1,0:T(8,128)(2,1)} %copy-done), calls=%async_computation.3 | async-start | bytes 9437184 | tf_op jit(solution)/shard_map/cond/branch_1_fun/all_to_all | solution.py:506
  331.3 17.7 %collective-permute-start.16 = (bf16[256,1024]{1,0:T(8,128)(2,1)S(1)}, bf16[256,1024]{1,0:T(8,128)(2,1)S(1)}, u32[]{:S(2)}, u32[]{:S(2)}) collective-permute-start(bf16[256,1024]{1,0:T(8,128)(2,1)S(1)} %slice.145), channel_id=1, source_target_pairs={{0,8},{2,10},{4,12},{6,14},{8,0},{10,2},{12,4},{14,6},{16,24},{18,... | collective-permute-start | bytes 1572872 | tf_op jit(solution)/shard_map/cond/branch_1_fun/ppermute | solution.py:20
  333.7 25.2 %collective-permute-start.14 = (bf16[256,1024]{1,0:T(8,128)(2,1)S(1)}, bf16[256,1024]{1,0:T(8,128)(2,1)S(1)}, u32[]{:S(2)}, u32[]{:S(2)}) collective-permute-start(bf16[256,1024]{1,0:T(8,128)(2,1)S(1)} %slice.119), channel_id=1, source_target_pairs={{0,8},{2,10},{4,12},{6,14},{8,0},{10,2},{12,4},{14,6},{16,24},{18,... | collective-permute-start | bytes 1572872 | tf_op jit(solution)/shard_map/cond/branch_1_fun/ppermute | solution.py:20
  349.3 14.7 %collective-permute-start.17 = (bf16[128,1024]{1,0:T(8,128)(2,1)S(1)}, bf16[128,1024]{1,0:T(8,128)(2,1)S(1)}, u32[]{:S(2)}, u32[]{:S(2)}) collective-permute-start(bf16[128,1024]{1,0:T(8,128)(2,1)S(1)} %slice.147), channel_id=1, source_target_pairs={{0,16},{2,18},{4,20},{6,22},{8,24},{10,26},{12,28},{14,30},{16,0},... | collective-permute-start | bytes 786440 | tf_op jit(solution)/shard_map/cond/branch_1_fun/ppermute | solution.py:20
  360.2 11.7 %collective-permute-start.15 = (bf16[128,1024]{1,0:T(8,128)(2,1)S(1)}, bf16[128,1024]{1,0:T(8,128)(2,1)S(1)}, u32[]{:S(2)}, u32[]{:S(2)}) collective-permute-start(bf16[128,1024]{1,0:T(8,128)(2,1)S(1)} %slice.143), channel_id=1, source_target_pairs={{0,16},{2,18},{4,20},{6,22},{8,24},{10,26},{12,28},{14,30},{16,0},... | collective-permute-start | bytes 786440 | tf_op jit(solution)/shard_map/cond/branch_1_fun/ppermute | solution.py:20
